TPU v7x, 512 devices: a whole 4x8x8 slice. The times are simulated.
512 devices in a mesh: row: 8 (over z), feat: 64 (over x, y, core).
Axes of the slice: x: 4, y: 8, z: 8, core: 2. Of those that a mesh axis runs over, the one named last changes fastest.
Arguments:
- logits: bfloat16 [32768, 1000], P(('row', 'feat')), may hold values from -200 to 200, as said below
- labels: int32 [32768], P(('row', 'feat')), may hold values from 0 to 999
- projection: bfloat16 [1000, 16], replicated, may hold values from -4 to 4
- bins: int32 [2048, 32768], P('feat', 'row'), may hold values from 0 to 63, as said below
- nbins: int32 [2048], P('feat'), may hold values from 2 to 64
- leaf: int32 [32768], P('row'), may hold values from 0 to 15
Outputs:
- relative_gain: float32 [16, 131072], P('row', 'feat')
Inputs may be any that keep to these rules, and one draw needn't show every extreme that they name: `logits`: shows the class scores; some rows may lie far from zero. bins[f, i] < nbins[f].
All inputs are finite; a program needn't handle non-finite values.
Results may differ from a plain program's by a relative error of at most 0.0017.
Values may be sent and summed in bfloat16 or wider, within the bound.
A program may use at most 64 MiB of HBM per device.

v0:
```python
import math

import jax
import jax.numpy as jnp
from jax import lax
from jax.sharding import PartitionSpec as P

BINS = 64
LEAVES = 16


ridge = 1.0
epsilon = 1e-06


def split_gains(histogram, nbins):
    left = jnp.cumsum(histogram, axis=3)
    total = left[..., -1:]
    right = total - left

    def score(sums):
        return jnp.sum(sums[:, :-1] * sums[:, :-1] / (sums[:, -1:] + ridge), axis=1)

    gain = score(left) + score(right) - score(total)
    valid = jnp.arange(histogram.shape[3], dtype=jnp.int32)[None, :] < nbins[:, None] - 1
    return jnp.where(valid[None], gain, jnp.zeros_like(gain))


def on_device(logits, labels, projection, bins, nbins, leaf):
    scores = logits.astype(jnp.float32)
    highest = jnp.max(scores, axis=1, keepdims=True)
    expd = jnp.exp(scores - highest)
    probability = expd / jnp.sum(expd, axis=1, keepdims=True)
    classes = jnp.arange(logits.shape[1], dtype=jnp.int32)
    target = (labels[:, None] == classes[None, :]).astype(jnp.float32)
    gradient = (probability - target).astype(jnp.bfloat16)
    sketch_cols = lax.dot_general(
        projection, gradient, (((0,), (1,)), ((), ())), preferred_element_type=jnp.float32
    )
    hessian = jnp.sum(probability * (1.0 - probability), axis=1)
    local_values = jnp.concatenate(
        [sketch_cols.astype(jnp.bfloat16), hessian.astype(jnp.bfloat16)[None, :]], axis=0
    )
    values = lax.all_gather(local_values, "feat", axis=1, tiled=True)
    columns = values.shape[0]
    rows = values.shape[1]
    leaf_hot = (leaf[:, None] == jnp.arange(LEAVES, dtype=jnp.int32)[None, :]).astype(jnp.bfloat16)
    weights = (leaf_hot[:, :, None] * values.T[:, None, :]).reshape(rows, LEAVES * columns)
    features = bins.shape[0]
    width = math.gcd(features, 8)
    groups = features // width
    span = width * BINS
    bin_values = jnp.arange(BINS, dtype=jnp.int32)

    def add_group(group_index, partial_value):
        group_bins = lax.dynamic_slice_in_dim(bins, group_index * width, width, 0)
        onehot = (
            (group_bins[:, None, :] == bin_values[None, :, None])
            .astype(jnp.bfloat16)
            .reshape(span, rows)
        )
        block = lax.dot_general(
            weights, onehot, (((0,), (1,)), ((), ())), preferred_element_type=jnp.float32
        )
        return lax.dynamic_update_slice_in_dim(partial_value, block, group_index * span, 1)

    partial_value = lax.fori_loop(
        0, groups, add_group, jnp.zeros((LEAVES * columns, features * BINS), jnp.float32)
    )
    share = LEAVES // lax.axis_size("row")
    summed = lax.psum(partial_value, "row")
    summed = lax.dynamic_slice_in_dim(
        summed, lax.axis_index("row") * share * columns, share * columns, 0
    )
    histogram = summed.reshape(share, columns, features, BINS)
    gain = split_gains(histogram, nbins)
    best = lax.pmax(jnp.max(gain, axis=(1, 2)), "feat")
    relative = gain / (best[:, None, None] + epsilon)
    return relative.reshape(share, features * BINS)


def solution(mesh):
    return jax.shard_map(
        on_device,
        mesh=mesh,
        in_specs=(
            P(("row", "feat"), None),
            P(("row", "feat")),
            P(),
            P("feat", "row"),
            P("feat"),
            P("row"),
        ),
        out_specs=P("row", "feat"),
        check_vma=False,
    )
```

profile of v0, /device:TPU:1, one launch (start us, length us, event | category | flops | bytes accessed | tf_op | source)
XLA Modules:
  0.0 334.5 jit_solution(5034517735450519379)
XLA Ops:
  6.5 0.0 copy-start
  6.5 0.0 copy-start.1
  6.5 0.0 all-reduce.2.cloned.1.call-start
  6.5 1.0 reduce_max.23
  7.6 1.1 fusion.14
  8.7 1.2 fusion.12
  9.9 0.0 copy-done
  9.9 1.2 fusion.5
  11.1 50.5 %all-gather = bf16[64,64,17]{1,2,0:T(8,128)(2,1)S(1)} all-gather(bf16[1,64,17]{1,2,0:T(8,128)(2,1)S(1)} %maximum_bitcast_fusion), channel_id=1, replica_groups=mesh['row'=8,'feat'=64] {'feat'}, dimensions={0}, use_global_device_ids=true | all-gather | bytes 141440 | tf_op jit(solution)/shard_map/all_gather | solution.py:44
  61.6 0.1 copy.12
  61.7 0.3 reshape.92
  61.9 0.0 copy-done.1
  62.0 1.6 broadcast_in_dim.20
  63.6 39.9 %while.14 = (s32[]{:T(128)}, f32[272,2048]{1,0:T(8,128)}, s32[32,4096]{1,0:T(8,128)}, bf16[4096,17]{0,1:T(8,128)(2,1)S(1)}, bf16[4096,16]{0,1:T(8,128)(2,1)S(1)}...) while((s32[]{:T(128)}, f32[272,2048]{1,0:T(8,128)}, ...), condition=%wide.region_4.0_spmd.clone, body=%wide.region_3.0_spmd.clone.sunk | while | flops 1144061952 | bytes 14336209 | solution.py:67
  63.6 0.9 constant_dynamic-slice_fusion.3
  64.5 0.1 eq.105
  64.6 2.3 bitcast_compare_fusion.2
  66.9 0.3 broadcast_multiply_fusion.2
  67.2 1.9 mul.106
  69.1 4.5 %fusion.27 = f32[272,2048]{1,0:T(8,128)} fusion(f32[272,2048]{1,0:T(8,128)} %get-tuple-element.172, s32[]{:T(128)S(6)} %select_n.33, pred[512,4096]{1,0:T(32,128)(4,1)} %bitcast_compare_fusion.2, bf16[4096,272]{0,1:T(8,128)(2,1)} %mul.106), kind=kOutput, calls=%fused_computation.5.clone.1 | convolution fusion | flops 1140850688 | bytes 4882436 | tf_op jit(solution)/shard_map/while/body/eval_jaxpr/dot_general | solution.py:62
  73.6 0.9 constant_dynamic-slice_fusion.3
  74.5 0.1 eq.105
  74.6 2.3 bitcast_compare_fusion.2
  76.9 0.3 broadcast_multiply_fusion.2
  77.2 1.9 mul.106
  79.1 4.5 %fusion.27 = f32[272,2048]{1,0:T(8,128)} fusion(f32[272,2048]{1,0:T(8,128)} %get-tuple-element.172, s32[]{:T(128)S(6)} %select_n.33, pred[512,4096]{1,0:T(32,128)(4,1)} %bitcast_compare_fusion.2, bf16[4096,272]{0,1:T(8,128)(2,1)} %mul.106), kind=kOutput, calls=%fused_computation.5.clone.1 | convolution fusion | flops 1140850688 | bytes 4882436 | tf_op jit(solution)/shard_map/while/body/eval_jaxpr/dot_general | solution.py:62
  83.6 0.9 constant_dynamic-slice_fusion.3
  84.5 0.1 eq.105
  84.6 2.3 bitcast_compare_fusion.2
  86.9 0.3 broadcast_multiply_fusion.2
  87.2 1.9 mul.106
  89.1 4.4 %fusion.27 = f32[272,2048]{1,0:T(8,128)} fusion(f32[272,2048]{1,0:T(8,128)} %get-tuple-element.172, s32[]{:T(128)S(6)} %select_n.33, pred[512,4096]{1,0:T(32,128)(4,1)} %bitcast_compare_fusion.2, bf16[4096,272]{0,1:T(8,128)(2,1)} %mul.106), kind=kOutput, calls=%fused_computation.5.clone.1 | convolution fusion | flops 1140850688 | bytes 4882436 | tf_op jit(solution)/shard_map/while/body/eval_jaxpr/dot_general | solution.py:62
  93.5 0.9 constant_dynamic-slice_fusion.3
  94.5 0.1 eq.105
  94.5 2.3 bitcast_compare_fusion.2
  96.8 0.3 broadcast_multiply_fusion.2
  97.1 1.9 mul.106
  99.0 4.5 %fusion.27 = f32[272,2048]{1,0:T(8,128)} fusion(f32[272,2048]{1,0:T(8,128)} %get-tuple-element.172, s32[]{:T(128)S(6)} %select_n.33, pred[512,4096]{1,0:T(32,128)(4,1)} %bitcast_compare_fusion.2, bf16[4096,272]{0,1:T(8,128)(2,1)} %mul.106), kind=kOutput, calls=%fused_computation.5.clone.1 | convolution fusion | flops 1140850688 | bytes 4882436 | tf_op jit(solution)/shard_map/while/body/eval_jaxpr/dot_general | solution.py:62
  103.5 0.0 copy-start.2
  103.5 0.0 all-reduce.2.cloned.1.call-update
  103.5 0.6 copy-done.2
  104.1 0.1 broadcast_reduce_fusion
  104.3 0.1 lt.53
  104.3 0.1 lt.51
  104.4 0.1 iota_compare_fusion.2
  104.5 84.4 %all-reduce.2.cloned.1.call-done = f32[272,2048]{1,0:T(8,128)} async-done(((f32[272,2048]{1,0:T(8,128)}), f32[272,2048]{1,0:T(8,128)}) %all-reduce.2.cloned.1.call-update) | async-done | bytes 2228240 | tf_op jit(solution)/shard_map/psum | solution.py:71
  188.9 1.0 constant_dynamic-slice_fusion.1
  189.9 0.2 reshape.90
  190.1 7.7 %reduce_window_sum.11 = f32[2,17,32,64]{3,2,1,0:T(8,128)S(1)} reduce-window(f32[2,17,32,64]{3,2,1,0:T(8,128)S(1)} %reshape.90, f32[]{:T(128)} %constant.65.clone.1), window={size=1x1x1x64 pad=0_0x0_0x0_0x63_0}, to_apply=%region_6.0 | reduce-window | flops 4386816 | bytes 557060 | tf_op jit(solution)/shard_map/jit(cumsum)/reduce_window_sum | solution.py:17
  197.8 0.2 slice.35
  198.0 0.2 fusion.16
  198.2 0.3 copy.13
  198.4 0.2 broadcast_subtract_fusion
  198.7 0.3 fusion.11
  199.0 0.2 fusion.9
  199.1 0.2 select_reduce_fusion
  199.3 0.1 sub.54
  199.4 127.6 %pmax.7 = f32[2]{0:T(128)S(1)} all-reduce(f32[2]{0:T(128)S(1)} %get-tuple-element.125), channel_id=1, replica_groups=mesh['row'=8,'feat'=64] {'feat'}, use_global_device_ids=true, to_apply=%region_11.12 | all-reduce | flops 2 | bytes 16 | tf_op jit(solution)/shard_map/pmax | solution.py:77
  327.0 0.7 select_divide_fusion
  (14 shorter events, 0.1 us)
Async XLA Ops:
  6.5 3.4 %copy-start = (bf16[1000,16]{0,1:T(8,128)(2,1)S(1)}, bf16[1000,16]{0,1:T(8,128)(2,1)}, u32[]{:S(2)}) copy-start(bf16[1000,16]{0,1:T(8,128)(2,1)} %param.10) | copy-start | bytes 96004
  6.5 55.4 %copy-start.1 = (s32[4096]{0:T(1024)S(1)}, s32[4096]{0:T(1024)}, u32[]{:S(2)}) copy-start(s32[4096]{0:T(1024)} %param.13) | copy-start | bytes 49156
  6.5 182.3 %all-reduce.2.cloned.1.call-start = ((), (), s32[]{:S(2)}) async-start(), calls=%async_computation | async-start | bytes 4456448 | tf_op jit(solution)/shard_map/psum | solution.py:71
  103.5 0.7 copy-start.2
Sparse Core Ops, SparseCore 0:
  103.6 85.1 all-reduce.1
where the time goes:
time: 335 us; the launch traced here: 334 us
  blocking collectives  178 us (53%)
  waiting for transfers between devices  84.4 us (25%)
  other arithmetic  23.1 us (7%)
  matrix products  19 us (6%)
  local copies, waits for them, and re-layouts  16.3 us (5%)
  between operations  13.5 us (4%)
    pmax x1, blocking collectives, on_device(): best = lax.pmax(jnp.max(gain, axis=(1, 2)), 'feat')  128 us
    psum x1, waiting for transfers between devices, on_device(): summed = lax.psum(partial_value, 'row')  84.4 us
    all_gather x1, blocking collectives, on_device(): values = lax.all_gather(local_values, 'feat', axis=1, tiled=True)  50.5 us
    dot_general x4, matrix products, add_group(): lax.dot_general(weights, onehot, (((0,), (1,)), ((), ())), preferred_elem...  17.9 us
    eq x4, other arithmetic, add_group(): group_bins[:, None, :] == bin_values[None, :, None]  9.22 us
    mul x4, local copies, waits for them, and re-layouts, on_device(): leaf_hot[:, :, None] * values.T[:, None, :]  7.67 us
    another operation x1, other arithmetic, split_gains(): left = jnp.cumsum(histogram, axis=3)  7.66 us
  transfers between devices with their start and end apart: 1, of which 1 were waited for; matrix products, arithmetic and copies ran while one was open for 0% of the time, Pallas kernels for 0%

commit v1 on v0

v1 whole, which is shorter than its diff:
```python
import functools

import jax
import jax.numpy as jnp
from jax import lax
from jax.experimental import pallas as pl
from jax.experimental.pallas import tpu as pltpu
from jax.sharding import PartitionSpec as P

BINS = 64
LEAVES = 16
K = 16
GROUP = 4
LANES = 128
MESH = pl.DeviceIdType.MESH
NT = (((1,), (1,)), ((), ()))

ridge = 1.0
epsilon = 1e-6


def near_first(t):
    return ((t + 1) // 2) * (2 * (t % 2) - 1)


def kernel(
    NX,
    NY,
    NZ,
    logits_any,
    labels_ref,
    proj_ref,
    bins_any,
    nbins_ref,
    leaf_ref,
    out_ref,
    logits_v,
    bins_v,
    grad,
    bins_s,
    leaf_s,
    zsk_s,
    zhs_s,
    bins_r,
    leaf_r,
    zsk_r,
    zhs_r,
    bins_f,
    leaf_f,
    sk,
    hs,
    weights,
    onehot,
    acc,
    hist_r,
    sums,
    gain_s,
    gain_r,
    max1_s,
    max1_r,
    max2_s,
    max2_r,
    max3_s,
    max3_r,
    local_sem,
    zs_sem,
    zr_sem,
    ys_sem,
    yr_sem,
    xs_sem,
    xr_sem,
    hist_sem,
    gs_sem,
    gr_sem,
    m1s_sem,
    m1r_sem,
    m2s_sem,
    m2r_sem,
    m3s_sem,
    m3r_sem,
):
    HZ = NZ // 2
    LP = LEAVES // NZ
    rows = labels_ref.shape[1]
    z = lax.axis_index("row")
    feat = lax.axis_index("feat")
    c = feat % 2
    y = (feat // 2) % NY
    x = feat // (2 * NY)
    h = z // HZ
    slot = (z % HZ) * 2 + c

    def dev(x_, y_, z_, c_):
        return (z_, (x_ * NY + y_) * 2 + c_)

    def remote(src, dst, send, recv, device):
        return pltpu.make_async_remote_copy(
            src_ref=src, dst_ref=dst, send_sem=send, recv_sem=recv, device_id=device, device_id_type=MESH
        )

    cp_logits = pltpu.make_async_copy(logits_any, logits_v, local_sem.at[0])
    cp_bins = pltpu.make_async_copy(bins_any, bins_v, local_sem.at[1])
    cp_logits.start()
    cp_bins.start()

    barrier = pltpu.get_barrier_semaphore()

    def greet(device):
        pl.semaphore_signal(barrier, inc=1, device_id=device, device_id_type=MESH)

    @pl.loop(1, 2 * NZ)
    def _(i):
        other = (z * 2 + c + i) % (2 * NZ)
        greet(dev(x, y, other // 2, other % 2))

    @pl.loop(1, NY)
    def _(i):
        greet(dev(x, (y + i) % NY, z, c))

    @pl.loop(1, NX)
    def _(i):
        greet(dev((x + i) % NX, y, z, c))
        greet(dev((x + i) % NX, y, z, 1 - c))

    with jax.named_scope("softmax"):
        cp_logits.wait()
        lane = lax.broadcasted_iota(jnp.int32, (rows, rows), 1)
        line = lax.broadcasted_iota(jnp.int32, (rows, rows), 0)
        spread = jnp.where(lane == line, labels_ref[...].astype(jnp.float32), 0.0)
        target = jnp.sum(spread, axis=1, keepdims=True).astype(jnp.int32)
        scores = logits_v[...].astype(jnp.float32)
        highest = jnp.max(scores, axis=1, keepdims=True)
        expd = jnp.exp(scores - highest)
        probability = expd * (1.0 / jnp.sum(expd, axis=1, keepdims=True))
        classes = lax.broadcasted_iota(jnp.int32, scores.shape, 1)
        gradient = probability - jnp.where(classes == target, 1.0, 0.0)
        grad[...] = jnp.zeros_like(grad)
        grad[pl.ds(pl.multiple_of(c * rows, rows), rows), :] = gradient.astype(jnp.bfloat16)
        sketch = lax.dot_general(proj_ref[...], grad[...], NT, preferred_element_type=jnp.float32)
        zsk_s[...] = sketch.astype(jnp.bfloat16)
        hessian = jnp.sum(probability * (1.0 - probability), axis=1, keepdims=True)
        hessian = hessian.astype(jnp.bfloat16).astype(jnp.float32)
        lane = lax.broadcasted_iota(jnp.int32, (rows, LANES), 1)
        line = lax.broadcasted_iota(jnp.int32, (rows, LANES), 0)
        zhs_s[...] = jnp.sum(jnp.where(lane == line + c * rows, hessian, 0.0), axis=0, keepdims=True)

    with jax.named_scope("barrier"):
        pl.semaphore_wait(barrier, 2 * NZ - 1 + NY - 1 + 2 * (NX - 1))

    def to_column(i, src, dst, kind, act):
        device = dev(x, y, (z + i) % NZ, h)
        send, recv = zs_sem.at[kind, i], zr_sem.at[kind, slot]
        here = (i == 0) & (c == h)

        @pl.when(here)
        def _():
            if act == "start":
                pltpu.make_async_copy(src, dst, recv).start()

        @pl.when(jnp.logical_not(here))
        def _():
            copy = remote(src, dst, send, recv, device)
            if act == "start":
                copy.start()
            else:
                copy.wait_send()

    def column_values(i, act):
        to_column(i, zsk_s, zsk_r.at[slot], 0, act)
        to_column(i, zhs_s, zhs_r.at[slot], 1, act)

    def column_bins(i, act):
        to_column(i, bins_s.at[(z + i) % NZ], bins_r.at[slot], 2, act)
        to_column(i, leaf_s, leaf_r.at[slot], 3, act)

    @pl.loop(0, NZ)
    def _(i):
        column_values(i, "start")

    with jax.named_scope("regroup"):
        cp_bins.wait()
        width = NY * LANES
        for d in range(NZ):
            four = bins_v[d * GROUP : (d + 1) * GROUP, :].astype(jnp.float32)
            bins_s[d] = jnp.concatenate(
                [four[:, i * width : (i + 1) * width] for i in range(NX)], axis=0
            ).astype(jnp.bfloat16)
        half = NX * NY // 2
        leaf_s[...] = leaf_ref[pl.ds(pl.multiple_of(c * half, half), half), :].astype(jnp.float32).astype(jnp.bfloat16)

    @pl.loop(0, NZ)
    def _(i):
        column_bins(i, "start")

    def block_copies(step, xs, ys, device, send, recv):
        return (
            remote(sk.at[xs, ys], sk.at[xs, ys], send.at[0, step], recv.at[0], device),
            remote(hs.at[xs, ys], hs.at[xs, ys], send.at[1, step], recv.at[1], device),
        )

    with jax.named_scope("zvalues"):
        lane = lax.broadcasted_iota(jnp.int32, (1, LANES), 1)
        first = lane < rows

        @pl.loop(0, 2 * HZ)
        def _(i):
            remote(zsk_s, zsk_r.at[i], zs_sem.at[0, 0], zr_sem.at[0, i], dev(x, y, z, c)).wait_recv()
            remote(zhs_s, zhs_r.at[i], zs_sem.at[0, 0], zr_sem.at[1, i], dev(x, y, z, c)).wait_recv()

        for i in range(HZ):
            span = slice(i * LANES, (i + 1) * LANES)
            sk[x, y, :, span] = jnp.where(
                first, zsk_r[2 * i].astype(jnp.float32), zsk_r[2 * i + 1].astype(jnp.float32)
            ).astype(jnp.bfloat16)
            hs[x, y, :, span] = jnp.where(first, zhs_r[2 * i], zhs_r[2 * i + 1])

    def y_copies(t):
        return block_copies(
            t, x, y, dev(x, (y + near_first(t) + NY) % NY, z, c), ys_sem, yr_sem.at[y]
        )

    def x_copies(i, ys):
        return block_copies(
            ys, x, ys, dev((x + i) % NX, y, z, c), xs_sem.at[i], xr_sem.at[x, ys]
        )

    @pl.loop(1, NY)
    def _(t):
        for copy in y_copies(t):
            copy.start()

    acc[...] = jnp.zeros_like(acc)

    with jax.named_scope("zbins"):
        for i in range(2 * HZ):
            remote(bins_s.at[0], bins_r.at[i], zs_sem.at[0, 0], zr_sem.at[2, i], dev(x, y, z, c)).wait_recv()
            remote(leaf_s, leaf_r.at[i], zs_sem.at[0, 0], zr_sem.at[3, i], dev(x, y, z, c)).wait_recv()
            for j in range(NY):
                bins_f[i, j] = bins_r[i, :, j * LANES : (j + 1) * LANES].astype(jnp.float32)
            leaf_f[i // 2, (i % 2) * half : (i % 2 + 1) * half] = leaf_r[i].astype(jnp.float32)

    bin_ids = lax.broadcasted_iota(jnp.int32, (BINS, LANES), 0).astype(jnp.float32).astype(jnp.bfloat16)
    leaf_ids = lax.broadcasted_iota(jnp.int32, (LEAVES, LANES), 0).astype(jnp.float32).astype(jnp.bfloat16)
    one, nil = jnp.bfloat16(1), jnp.bfloat16(0)

    def add_block(xs, ys):
        for i in range(HZ):
            span = slice(i * LANES, (i + 1) * LANES)
            leaf = leaf_f[i, pl.ds(xs * NY + ys, 1), :]
            leaf = jnp.broadcast_to(leaf, (LEAVES, LANES)).astype(jnp.bfloat16)
            tile = sk[xs, ys, :, span]
            for l in range(LEAVES):
                weights[l * K : (l + 1) * K, span] = jnp.where(leaf == jnp.bfloat16(l), tile, nil)
            hess = jnp.broadcast_to(hs[xs, ys, :, span], (LEAVES, LANES)).astype(jnp.bfloat16)
            weights[LEAVES * K :, span] = jnp.where(leaf == leaf_ids, hess, nil)
            for side in range(2):
                for f in range(GROUP):
                    ids = bins_f[2 * i + side, ys, pl.ds(xs * GROUP + f, 1), :]
                    ids = jnp.broadcast_to(ids, (BINS, LANES)).astype(jnp.bfloat16)
                    onehot[side, f * BINS : (f + 1) * BINS, span] = jnp.where(ids == bin_ids, one, nil)
        for side in range(2):
            acc[side] += lax.dot_general(weights[...], onehot[side], NT, preferred_element_type=jnp.float32)

    def forward(ys):
        @pl.loop(1, NX)
        def _(i):
            for copy in x_copies(i, ys):
                copy.start()

    with jax.named_scope("ownslab"):

        @pl.loop(0, NY)
        def _(t):
            ys = (y + near_first(t) + NY) % NY

            @pl.when(t > 0)
            def _():
                for copy in block_copies(t, x, ys, dev(x, y, z, c), ys_sem, yr_sem.at[ys]):
                    copy.wait_recv()

            forward(ys)
            add_block(x, ys)

    with jax.named_scope("slabs"):

        @pl.loop(0, NY * (NX - 1))
        def _(t):
            ys = (y + near_first(t // (NX - 1)) + NY) % NY
            xs = (x + near_first(t % (NX - 1) + 1) + NX) % NX
            for copy in block_copies(ys, xs, ys, dev(x, y, z, c), xs_sem.at[1], xr_sem.at[xs, ys]):
                copy.wait_recv()
            add_block(xs, ys)

    with jax.named_scope("cores"):
        swap = remote(acc.at[1 - c], hist_r, hist_sem.at[0], hist_sem.at[1], dev(x, y, z, 1 - c))
        swap.start()
        swap.wait_recv()

    with jax.named_scope("gains"):
        hist = acc[c] + hist_r[...]
        cols = GROUP * BINS
        src = lax.broadcasted_iota(jnp.int32, (cols, cols), 0)
        dst = lax.broadcasted_iota(jnp.int32, (cols, cols), 1)
        same = (src // BINS) == (dst // BINS)
        upto = jnp.where(same & (src <= dst), 1.0, 0.0).astype(jnp.bfloat16)
        past = jnp.where(same & (src > dst), 1.0, 0.0).astype(jnp.bfloat16)
        left = jnp.zeros_like(hist)
        right = jnp.zeros_like(hist)
        rest = hist
        for _ in range(3):
            piece = rest.astype(jnp.bfloat16)
            rest = rest - piece.astype(jnp.float32)
            left += jnp.dot(piece, upto, preferred_element_type=jnp.float32)
            right += jnp.dot(piece, past, preferred_element_type=jnp.float32)
        for i in range(cols // LANES):
            sums[0, i] = left[:, i * LANES : (i + 1) * LANES]
            sums[1, i] = right[:, i * LANES : (i + 1) * LANES]

        def side_sums(side, lines):
            return jnp.concatenate([sums[side, i, lines, :] for i in range(cols // LANES)], axis=1)

        def squares(get):
            total = jnp.zeros((LEAVES, cols), jnp.float32)
            for k in range(K):
                s = get(pl.ds(k, LEAVES, stride=K))
                total += s * s
            return total / (get(slice(LEAVES * K, LEAVES * K + LEAVES)) + ridge)

        gain = (
            squares(lambda r: side_sums(0, r))
            + squares(lambda r: side_sums(1, r))
            - squares(lambda r: side_sums(0, r) + side_sums(1, r))
        )
        lane = lax.broadcasted_iota(jnp.int32, (1, cols), 1)
        counts = jnp.zeros((1, cols), jnp.int32)
        for f in range(GROUP):
            counts = jnp.where(lane // BINS == f, nbins_ref[z * GROUP + f], counts)
        gain = jnp.where(lane % BINS < counts - 1, gain, 0.0)
        for i in range(NZ):
            gain_s[i] = gain[i * LP : (i + 1) * LP]
        best = jnp.max(gain, axis=1, keepdims=True)
        max1_s[...] = jnp.broadcast_to(best, (LEAVES, LANES))

    def gain_copy(i):
        other = (z + i) % NZ
        return remote(gain_s.at[other], gain_r.at[z], gs_sem.at[i], gr_sem.at[z], dev(x, y, other, c))

    def max1_copy(i):
        return remote(max1_s, max1_r.at[y], m1s_sem.at[i], m1r_sem.at[y], dev(x, (y + i) % NY, z, c))

    mine = x * 2 + c

    def max2_copy(i):
        other = (mine + i) % (2 * NX)
        return remote(max2_s, max2_r.at[mine], m2s_sem.at[i], m2r_sem.at[mine], dev(other // 2, y, z, other % 2))

    def max3_copy(i):
        other = (z + i) % NZ
        return remote(max3_s.at[other], max3_r.at[z], m3s_sem.at[i], m3r_sem.at[z], dev(x, y, other, c))

    with jax.named_scope("max1"):

        @pl.loop(1, NY)
        def _(i):
            max1_copy(i).start()

        @pl.loop(1, NZ)
        def _(i):
            gain_copy(i).start()

        best = max1_s[...]
        max1_r[y] = best

        @pl.loop(1, NY)
        def _(i):
            other = (y + i) % NY
            remote(max1_s, max1_r.at[other], m1s_sem.at[0], m1r_sem.at[other], dev(x, y, z, c)).wait_recv()

        max2_s[...] = functools.reduce(jnp.maximum, [max1_r[i] for i in range(NY)])

    with jax.named_scope("max2"):

        @pl.loop(1, 2 * NX)
        def _(i):
            max2_copy(i).start()

        max2_r[mine] = max2_s[...]

        @pl.loop(1, 2 * NX)
        def _(i):
            other = (mine + i) % (2 * NX)
            remote(max2_s, max2_r.at[other], m2s_sem.at[0], m2r_sem.at[other], dev(x, y, z, c)).wait_recv()

        best = functools.reduce(jnp.maximum, [max2_r[i] for i in range(2 * NX)])
        for i in range(NZ):
            max3_s[i] = best[i * LP : (i + 1) * LP]

    with jax.named_scope("max3"):

        @pl.loop(1, NZ)
        def _(i):
            max3_copy(i).start()

        max3_r[z] = max3_s[z]
        gain_r[z] = gain_s[z]

        @pl.loop(1, NZ)
        def _(i):
            other = (z + i) % NZ
            remote(gain_s.at[0], gain_r.at[other], gs_sem.at[0], gr_sem.at[other], dev(x, y, z, c)).wait_recv()
            remote(max3_s.at[0], max3_r.at[other], m3s_sem.at[0], m3r_sem.at[other], dev(x, y, z, c)).wait_recv()

        best = functools.reduce(jnp.maximum, [max3_r[i] for i in range(NZ)])[:, :1]
        for i in range(NZ):
            out_ref[:, i * cols : (i + 1) * cols] = gain_r[i] / (best + epsilon)

    with jax.named_scope("sends"):

        @pl.loop(0, NZ)
        def _(i):
            column_values(i, "wait")
            column_bins(i, "wait")

        @pl.loop(1, NY)
        def _(t):
            for copy in y_copies(t):
                copy.wait_send()

        @pl.loop(0, NY)
        def _(t):
            @pl.loop(1, NX)
            def _(i):
                for copy in x_copies(i, t):
                    copy.wait_send()

        swap.wait_send()

        @pl.loop(1, NZ)
        def _(i):
            gain_copy(i).wait_send()
            max3_copy(i).wait_send()

        @pl.loop(1, NY)
        def _(i):
            max1_copy(i).wait_send()

        @pl.loop(1, 2 * NX)
        def _(i):
            max2_copy(i).wait_send()


def on_device(NX, NY, NZ, logits, labels, projection, bins, nbins, leaf):
    bf16, f32 = jnp.bfloat16, jnp.float32
    HZ = NZ // 2
    LP = LEAVES // NZ
    rows, classes = logits.shape
    span = HZ * LANES
    cols = GROUP * BINS
    tall = LEAVES * (K + 1)
    VMEM, DMA = pltpu.VMEM, pltpu.SemaphoreType.DMA
    vmem = pl.BlockSpec(memory_space=pltpu.VMEM)
    smem = pl.BlockSpec(memory_space=pltpu.SMEM)
    hbm = pl.BlockSpec(memory_space=pl.ANY)
    half = NX * NY // 2
    bin_block = (GROUP * NX, NY * LANES)
    return pl.pallas_call(
        functools.partial(kernel, NX, NY, NZ),
        out_shape=jax.ShapeDtypeStruct((LP, NZ * cols), f32),
        in_specs=[hbm, vmem, vmem, hbm, smem, vmem],
        out_specs=vmem,
        scratch_shapes=[
            VMEM(logits.shape, bf16),
            VMEM(bins.shape, jnp.int32),
            VMEM((2 * rows, classes), bf16),
            VMEM((NZ, *bin_block), bf16),
            VMEM((half, LANES), bf16),
            VMEM((K, LANES), bf16),
            VMEM((1, LANES), f32),
            VMEM((NZ, *bin_block), bf16),
            VMEM((NZ, half, LANES), bf16),
            VMEM((NZ, K, LANES), bf16),
            VMEM((NZ, 1, LANES), f32),
            VMEM((NZ, NY, GROUP * NX, LANES), f32),
            VMEM((HZ, 2 * half, LANES), f32),
            VMEM((NX, NY, K, span), bf16),
            VMEM((NX, NY, 1, span), f32),
            VMEM((tall, span), bf16),
            VMEM((2, cols, span), bf16),
            VMEM((2, tall, cols), f32),
            VMEM((tall, cols), f32),
            VMEM((2, cols // LANES, tall, LANES), f32),
            VMEM((NZ, LP, cols), f32),
            VMEM((NZ, LP, cols), f32),
            VMEM((LEAVES, LANES), f32),
            VMEM((NY, LEAVES, LANES), f32),
            VMEM((LEAVES, LANES), f32),
            VMEM((2 * NX, LEAVES, LANES), f32),
            VMEM((NZ, LP, LANES), f32),
            VMEM((NZ, LP, LANES), f32),
            DMA((2,)),
            DMA((4, NZ)),
            DMA((4, NZ)),
            DMA((2, NY)),
            DMA((NY, 2)),
            DMA((NX, 2, NY)),
            DMA((NX, NY, 2)),
            DMA((2,)),
            DMA((NZ,)),
            DMA((NZ,)),
            DMA((NY,)),
            DMA((NY,)),
            DMA((2 * NX,)),
            DMA((2 * NX,)),
            DMA((NZ,)),
            DMA((NZ,)),
        ],
        compiler_params=pltpu.CompilerParams(
            collective_id=0, has_side_effects=True, vmem_limit_bytes=40 * 2**20
        ),
        cost_estimate=pl.CostEstimate(
            flops=2 * tall * 2 * cols * NX * NY * span, bytes_accessed=2**20, transcendentals=rows * classes
        ),
    )(
        logits,
        labels.reshape(1, rows),
        projection.T,
        bins,
        nbins,
        leaf.reshape(2 * half, LANES),
    )


def solution(mesh, NX=4, NY=8):
    return jax.shard_map(
        functools.partial(on_device, NX, NY, mesh.shape["row"]),
        mesh=mesh,
        in_specs=(
            P(("row", "feat"), None),
            P(("row", "feat")),
            P(),
            P("feat", "row"),
            P("feat"),
            P("row"),
        ),
        out_specs=P("row", "feat"),
        check_vma=False,
    )
```

time: 335 us -> 63.2 us (0.19)
  blocking collectives: 178 us -> 0 us
  waiting for transfers between devices: 84.4 us -> 0 us
  Pallas kernels: 0 us -> 58.2 us
  other arithmetic: 23.1 us -> 0 us
  matrix products: 19 us -> 0 us
  between operations: 13.5 us -> 0.02 us
  local copies, waits for them, and re-layouts: 16.3 us -> 4.7 us
    pmax x1 -> x0, blocking collectives: 128 us -> none  [on_device(): best = lax.pmax(jnp.max(gain, axis=(1, 2)), 'feat')]
    psum x1 -> x0, waiting for transfers between devices: 84.4 us -> none  [on_device(): summed = lax.psum(partial_value, 'row')]
    pallas_call x0 -> x1, Pallas kernels: none -> 58.2 us  [on_device(): pl.pallas_call(functools.partial(kernel, NX, NY, NZ), out_shape=jax.Shape...]
    all_gather x1 -> x0, blocking collectives: 50.5 us -> none  [on_device(): values = lax.all_gather(local_values, 'feat', axis=1, tiled=True)]
    dot_general x5 -> x0, matrix products: 19 us -> none  [the longest x4 17.9 us: add_group(): lax.dot_general(weights, onehot, (((0,), (1,)), ((), ())), preferred_elem...]
    eq x4 -> x0, other arithmetic: 9.22 us -> none  [add_group(): group_bins[:, None, :] == bin_values[None, :, None]]
    mul x4 -> x0, local copies, waits for them, and re-layouts: 7.67 us -> none  [on_device(): leaf_hot[:, :, None] * values.T[:, None, :]]
    another operation x1 -> x0, other arithmetic: 7.66 us -> none  [split_gains(): left = jnp.cumsum(histogram, axis=3)]
  transfers between devices with their start and end apart: 1 -> 0, of which waited for: 1 -> 0; matrix products, arithmetic and copies ran while one was open for 0% -> 0% of each run, Pallas kernels for 0% -> 0%
where the time goes in v1:
time: 63.2 us; the launch traced here: 62.9 us
  Pallas kernels  58.2 us (92%)
  local copies, waits for them, and re-layouts  4.7 us (7%)
    pallas_call x1, Pallas kernels, on_device(): pl.pallas_call(functools.partial(kernel, NX, NY, NZ), out_shape=jax.Shape...  58.2 us
    unnamed x13, local copies, waits for them, and re-layouts  4.7 us

profile of v1, /device:TPU:1, one launch (start us, length us, event | category | flops | bytes accessed | tf_op | source)
XLA Modules:
  0.0 62.9 jit_solution(16440927017280131513)
XLA Ops:
  0.0 0.0 copy-start.4
  0.0 0.0 copy-start.5
  0.0 0.7 %copy-done.4 = s32[64]{0:T(128)S(1)} copy-done((s32[64]{0:T(128)S(1)}, s32[64]{0:T(128)}, u32[]{:S(2)}) %copy-start.4) | copy-done | bytes 280
  0.7 0.0 copy-done.5
  0.7 0.0 copy-start
  0.7 1.0 %copy-done = s32[32,4096]{1,0:T(8,128)S(1)} copy-done((s32[32,4096]{1,0:T(8,128)S(1)}, s32[32,4096]{1,0:T(8,128)}, u32[]{:S(2)}) %copy-start) | copy-done | bytes 524312
  1.7 0.0 copy-start.1
  1.7 0.9 %copy-done.1 = bf16[64,1000]{1,0:T(8,128)(2,1)S(1)} copy-done((bf16[64,1000]{1,0:T(8,128)(2,1)S(1)}, bf16[64,1000]{1,0:T(8,128)(2,1)}, u32[]{:S(2)}) %copy-start.1) | copy-done | bytes 128024
  2.6 0.0 copy-start.2
  2.6 0.8 %copy-done.2 = bf16[1000,16]{0,1:T(8,128)(2,1)S(1)} copy-done((bf16[1000,16]{0,1:T(8,128)(2,1)S(1)}, bf16[1000,16]{0,1:T(8,128)(2,1)}, u32[]{:S(2)}) %copy-start.2) | copy-done | bytes 32024
  3.4 0.0 copy-start.3
  3.4 0.7 %copy-done.3 = s32[4096]{0:T(1024)S(1)} copy-done((s32[4096]{0:T(1024)S(1)}, s32[4096]{0:T(1024)}, u32[]{:S(2)}) %copy-start.3) | copy-done | bytes 16408
  4.1 58.2 %shard_map.64 = f32[2,2048]{1,0:T(2,128)S(1)} custom-call(bf16[64,1000]{1,0:T(8,128)(2,1)S(1)} %copy-done.1, s32[1,64]{1,0:T(1,128)S(1)} %bitcast.5, bf16[16,1000]{1,0:T(8,128)(2,1)S(1)} %bitcast.3, s32[32,4096]{1,0:T(8,128)S(1)} %copy-done, s32[32]{0:T(128)S(1)} %copy-done.5, s32[32,128]{1,0:T(8,128)S(1)} %bitcast.4), custom_call_target="tpu_custom_call" | custom-call | flops 4563402752 | bytes 1048576 | tf_op jit(solution)/shard_map/pallas_call | solution.py:466
  62.3 0.6 copy.8
Async XLA Ops:
  0.0 0.7 %copy-start.4 = (s32[64]{0:T(128)S(1)}, s32[64]{0:T(128)}, u32[]{:S(2)}) copy-start(s32[64]{0:T(128)} %param.7) | copy-start | bytes 772
  0.0 0.7 %copy-start.5 = (s32[32]{0:T(128)S(1)}, s32[32]{0:T(128)}, u32[]{:S(2)}) copy-start(s32[32]{0:T(128)} %nbins_ref.1) | copy-start | bytes 388
  0.7 1.0 %copy-start = (s32[32,4096]{1,0:T(8,128)S(1)}, s32[32,4096]{1,0:T(8,128)}, u32[]{:S(2)}) copy-start(s32[32,4096]{1,0:T(8,128)} %bins_any.1) | copy-start | bytes 1572868
  1.7 0.9 %copy-start.1 = (bf16[64,1000]{1,0:T(8,128)(2,1)S(1)}, bf16[64,1000]{1,0:T(8,128)(2,1)}, u32[]{:S(2)}) copy-start(bf16[64,1000]{1,0:T(8,128)(2,1)} %logits_any.1) | copy-start | bytes 384004
  2.6 0.8 %copy-start.2 = (bf16[1000,16]{0,1:T(8,128)(2,1)S(1)}, bf16[1000,16]{0,1:T(8,128)(2,1)}, u32[]{:S(2)}) copy-start(bf16[1000,16]{0,1:T(8,128)(2,1)} %param.8) | copy-start | bytes 96004
  3.4 0.7 %copy-start.3 = (s32[4096]{0:T(1024)S(1)}, s32[4096]{0:T(1024)}, u32[]{:S(2)}) copy-start(s32[4096]{0:T(1024)} %param.11) | copy-start | bytes 49156

commit v2 on v1

v2 whole, which is shorter than its diff:
```python
import functools

import jax
import jax.numpy as jnp
from jax import lax
from jax.experimental import pallas as pl
from jax.experimental.pallas import tpu as pltpu
from jax.sharding import PartitionSpec as P

BINS = 64
LEAVES = 16
K = 16
GROUP = 4
QUAD = 4
LANES = 128
MESH = pl.DeviceIdType.MESH
NT = (((1,), (1,)), ((), ()))

ridge = 1.0
epsilon = 1e-6


def near_first(t):
    return ((t + 1) // 2) * (2 * (t % 2) - 1)


def far_first(t, n):
    return n // 2 + near_first(t)


def kernel(
    NX,
    NY,
    NZ,
    logits_any,
    labels_any,
    proj_any,
    bins_any,
    nbins_any,
    leaf_any,
    out_ref,
    logits_v,
    labels_ref,
    proj_ref,
    bins_v,
    nbins_ref,
    leaf_ref,
    grad,
    bins_s,
    leaf_s,
    zsk_s,
    zhs_s,
    bins_r,
    leaf_r,
    zsk_r,
    zhs_r,
    bins_f,
    leaf_f,
    sk,
    hs,
    weights,
    onehot,
    acc,
    hist_r,
    sums,
    gain_s,
    gain_r,
    pair_s,
    pair_r,
    best_s,
    best_r,
    local_sem,
    zs_sem,
    zr_sem,
    ys_sem,
    yr_sem,
    xs_sem,
    xr_sem,
    hist_sem,
    gs_sem,
    gr_sem,
    pair_sem,
    bs_sem,
    br_sem,
):
    HZ = NZ // 2
    LP = LEAVES // NZ
    rows = labels_ref.shape[1]
    z = lax.axis_index("row")
    feat = lax.axis_index("feat")
    c = feat % 2
    y = (feat // 2) % NY
    x = feat // (2 * NY)
    h = z // HZ
    slot = (z % HZ) * 2 + c

    def dev(x_, y_, z_, c_):
        return (z_, (x_ * NY + y_) * 2 + c_)

    def remote(src, dst, send, recv, device):
        return pltpu.make_async_remote_copy(
            src_ref=src, dst_ref=dst, send_sem=send, recv_sem=recv, device_id=device, device_id_type=MESH
        )

    operands = (
        (bins_any, bins_v),
        (logits_any, logits_v),
        (labels_any, labels_ref),
        (proj_any, proj_ref),
        (leaf_any, leaf_ref),
        (nbins_any, nbins_ref),
    )
    fetches = [pltpu.make_async_copy(src, dst, local_sem.at[i]) for i, (src, dst) in enumerate(operands)]
    for fetch in fetches:
        fetch.start()

    barrier = pltpu.get_barrier_semaphore()

    def greet(device):
        pl.semaphore_signal(barrier, inc=1, device_id=device, device_id_type=MESH)

    @pl.loop(1, 2 * NZ)
    def _(i):
        other = (z * 2 + c + i) % (2 * NZ)
        greet(dev(x, y, other // 2, other % 2))

    @pl.loop(1, NY)
    def _(i):
        greet(dev(x, (y + i) % NY, z, c))

    @pl.loop(1, NX)
    def _(i):
        greet(dev((x + i) % NX, y, z, c))

    with jax.named_scope("softmax"):
        for fetch in fetches[1:4]:
            fetch.wait()
        lane = lax.broadcasted_iota(jnp.int32, (rows, rows), 1)
        line = lax.broadcasted_iota(jnp.int32, (rows, rows), 0)
        spread = jnp.where(lane == line, labels_ref[...].astype(jnp.float32), 0.0)
        target = jnp.sum(spread, axis=1, keepdims=True).astype(jnp.int32)
        scores = logits_v[...].astype(jnp.float32)
        highest = jnp.max(scores, axis=1, keepdims=True)
        expd = jnp.exp(scores - highest)
        probability = expd * (1.0 / jnp.sum(expd, axis=1, keepdims=True))
        classes = lax.broadcasted_iota(jnp.int32, scores.shape, 1)
        gradient = probability - jnp.where(classes == target, 1.0, 0.0)
        grad[...] = jnp.zeros_like(grad)
        grad[pl.ds(pl.multiple_of(c * rows, rows), rows), :] = gradient.astype(jnp.bfloat16)
        sketch = lax.dot_general(proj_ref[...], grad[...], NT, preferred_element_type=jnp.float32)
        zsk_s[...] = sketch.astype(jnp.bfloat16)
        hessian = jnp.sum(probability * (1.0 - probability), axis=1, keepdims=True)
        hessian = hessian.astype(jnp.bfloat16).astype(jnp.float32)
        lane = lax.broadcasted_iota(jnp.int32, (rows, LANES), 1)
        line = lax.broadcasted_iota(jnp.int32, (rows, LANES), 0)
        zhs_s[...] = jnp.sum(jnp.where(lane == line + c * rows, hessian, 0.0), axis=0, keepdims=True)

    with jax.named_scope("barrier"):
        pl.semaphore_wait(barrier, 2 * NZ - 1 + NY - 1 + NX - 1)

    def to_column(t, src, dst, kind, act):
        device = dev(x, y, (z + far_first(t, NZ)) % NZ, h)
        send, recv = zs_sem.at[kind, t], zr_sem.at[kind, slot]
        here = (t == NZ - 1) & (c == h)

        @pl.when(here)
        def _():
            if act == "start":
                pltpu.make_async_copy(src, dst, recv).start()

        @pl.when(jnp.logical_not(here))
        def _():
            copy = remote(src, dst, send, recv, device)
            if act == "start":
                copy.start()
            else:
                copy.wait_send()

    def column_values(i, act):
        to_column(i, zsk_s, zsk_r.at[slot], 0, act)
        to_column(i, zhs_s, zhs_r.at[slot], 1, act)

    def column_bins(i, act):
        to_column(i, bins_s.at[(z + far_first(i, NZ)) % NZ], bins_r.at[slot], 2, act)
        to_column(i, leaf_s, leaf_r.at[slot], 3, act)

    @pl.loop(0, NZ)
    def _(i):
        column_values(i, "start")

    with jax.named_scope("regroup"):
        fetches[0].wait()
        fetches[4].wait()
        width = NY * LANES
        for d in range(NZ):
            four = bins_v[d * GROUP : (d + 1) * GROUP, :].astype(jnp.float32)
            bins_s[d] = jnp.concatenate(
                [four[:, i * width : (i + 1) * width] for i in range(NX)], axis=0
            ).astype(jnp.bfloat16)
        half = NX * NY // 2
        leaf_s[...] = leaf_ref[pl.ds(pl.multiple_of(c * half, half), half), :].astype(jnp.float32).astype(jnp.bfloat16)

    @pl.loop(0, NZ)
    def _(i):
        column_bins(i, "start")

    def block_copies(step, xs, ys, device, send, recv):
        return (
            remote(sk.at[xs, ys], sk.at[xs, ys], send.at[0, step], recv.at[0], device),
            remote(hs.at[xs, ys], hs.at[xs, ys], send.at[1, step], recv.at[1], device),
        )

    with jax.named_scope("zvalues"):
        lane = lax.broadcasted_iota(jnp.int32, (1, LANES), 1)
        first = lane < rows

        @pl.loop(0, 2 * HZ)
        def _(i):
            remote(zsk_s, zsk_r.at[i], zs_sem.at[0, 0], zr_sem.at[0, i], dev(x, y, z, c)).wait_recv()
            remote(zhs_s, zhs_r.at[i], zs_sem.at[0, 0], zr_sem.at[1, i], dev(x, y, z, c)).wait_recv()

        for i in range(HZ):
            span = slice(i * LANES, (i + 1) * LANES)
            sk[x, y, :, span] = jnp.where(
                first, zsk_r[2 * i].astype(jnp.float32), zsk_r[2 * i + 1].astype(jnp.float32)
            ).astype(jnp.bfloat16)
            hs[x, y, :, span] = jnp.where(first, zhs_r[2 * i], zhs_r[2 * i + 1])

    def y_copies(t):
        device = dev(x, (y + far_first(t, NY)) % NY, z, c)
        return block_copies(t, x, y, device, ys_sem, yr_sem.at[y])

    def x_copies(t, ys):
        device = dev((x + far_first(t, NX)) % NX, y, z, c)
        return block_copies(ys, x, ys, device, xs_sem.at[t], xr_sem.at[x, ys])

    def forward(ys):
        @pl.loop(0, NX - 1)
        def _(t):
            for copy in x_copies(t, ys):
                copy.start()

    @pl.loop(0, NY - 1)
    def _(t):
        for copy in y_copies(t):
            copy.start()

    forward(y)
    acc[...] = jnp.zeros_like(acc)

    def near_y(t):
        return (y + near_first(t) + NY) % NY

    def await_y(t):
        ys = near_y(t)
        for copy in block_copies(0, x, ys, dev(x, y, z, c), ys_sem, yr_sem.at[ys]):
            copy.wait_recv()
        forward(ys)

    pl.loop(1, QUAD)(await_y)

    with jax.named_scope("zbins"):
        for i in range(2 * HZ):
            remote(bins_s.at[0], bins_r.at[i], zs_sem.at[0, 0], zr_sem.at[2, i], dev(x, y, z, c)).wait_recv()
            remote(leaf_s, leaf_r.at[i], zs_sem.at[0, 0], zr_sem.at[3, i], dev(x, y, z, c)).wait_recv()
            for j in range(NY):
                bins_f[i, j] = bins_r[i, :, j * LANES : (j + 1) * LANES].astype(jnp.float32)
            leaf_f[i // 2, (i % 2) * half : (i % 2 + 1) * half] = leaf_r[i].astype(jnp.float32)

    bin_ids = lax.broadcasted_iota(jnp.int32, (BINS, LANES), 0).astype(jnp.float32).astype(jnp.bfloat16)
    leaf_ids = lax.broadcasted_iota(jnp.int32, (LEAVES, LANES), 0).astype(jnp.float32).astype(jnp.bfloat16)
    one, nil = jnp.bfloat16(1), jnp.bfloat16(0)

    def build(xs, quad):
        for b in range(QUAD):
            ys = near_y(quad * QUAD + b)
            for i in range(HZ):
                src = slice(i * LANES, (i + 1) * LANES)
                dst = slice((b * HZ + i) * LANES, (b * HZ + i + 1) * LANES)
                leaf = leaf_f[i, pl.ds(xs * NY + ys, 1), :]
                leaf = jnp.broadcast_to(leaf, (LEAVES, LANES)).astype(jnp.bfloat16)
                tile = sk[xs, ys, :, src]
                for l in range(LEAVES):
                    weights[l * K : (l + 1) * K, dst] = jnp.where(leaf == jnp.bfloat16(l), tile, nil)
                hess = jnp.broadcast_to(hs[xs, ys, :, src], (LEAVES, LANES)).astype(jnp.bfloat16)
                weights[LEAVES * K :, dst] = jnp.where(leaf == leaf_ids, hess, nil)
                for side in range(2):
                    for f in range(GROUP):
                        ids = bins_f[2 * i + side, ys, pl.ds(xs * GROUP + f, 1), :]
                        ids = jnp.broadcast_to(ids, (BINS, LANES)).astype(jnp.bfloat16)
                        onehot[side, f * BINS : (f + 1) * BINS, dst] = jnp.where(ids == bin_ids, one, nil)

    def add_side(side):
        acc[side] += lax.dot_general(weights[...], onehot[side], NT, preferred_element_type=jnp.float32)

    def add_quad(xs, quad):
        build(xs, quad)
        add_side(0)
        add_side(1)

    with jax.named_scope("ownslab"):

        @pl.loop(0, NY // QUAD)
        def _(quad):
            @pl.when(quad > 0)
            def _():
                pl.loop(quad * QUAD, (quad + 1) * QUAD)(await_y)

            add_quad(x, quad)

    def await_x(t):
        quad, xs = t // (NX - 1), (x + near_first(t % (NX - 1) + 1) + NX) % NX

        @pl.loop(quad * QUAD, (quad + 1) * QUAD)
        def _(i):
            ys = near_y(i)
            for copy in block_copies(0, xs, ys, dev(x, y, z, c), xs_sem.at[0], xr_sem.at[xs, ys]):
                copy.wait_recv()

        return xs, quad

    swap = remote(acc.at[1 - c], hist_r, hist_sem.at[0], hist_sem.at[1], dev(x, y, z, 1 - c))
    n_quads = (NX - 1) * (NY // QUAD)

    with jax.named_scope("slabs"):

        @pl.loop(0, n_quads - 1)
        def _(t):
            add_quad(*await_x(t))

        build(*await_x(n_quads - 1))
        add_side(1 - c)
        swap.start()
        add_side(c)

    with jax.named_scope("cores"):
        swap.wait_recv()

    with jax.named_scope("gains"):
        hist = acc[c] + hist_r[...]
        cols = GROUP * BINS
        src = lax.broadcasted_iota(jnp.int32, (cols, cols), 0)
        dst = lax.broadcasted_iota(jnp.int32, (cols, cols), 1)
        same = (src // BINS) == (dst // BINS)
        upto = jnp.where(same & (src <= dst), 1.0, 0.0).astype(jnp.bfloat16)
        past = jnp.where(same & (src > dst), 1.0, 0.0).astype(jnp.bfloat16)
        left = jnp.zeros_like(hist)
        right = jnp.zeros_like(hist)
        rest = hist
        for _ in range(3):
            piece = rest.astype(jnp.bfloat16)
            rest = rest - piece.astype(jnp.float32)
            left += jnp.dot(piece, upto, preferred_element_type=jnp.float32)
            right += jnp.dot(piece, past, preferred_element_type=jnp.float32)
        for i in range(cols // LANES):
            sums[0, i] = left[:, i * LANES : (i + 1) * LANES]
            sums[1, i] = right[:, i * LANES : (i + 1) * LANES]

        def side_sums(side, lines):
            return jnp.concatenate([sums[side, i, lines, :] for i in range(cols // LANES)], axis=1)

        def squares(get):
            total = jnp.zeros((LEAVES, cols), jnp.float32)
            for k in range(K):
                s = get(pl.ds(k, LEAVES, stride=K))
                total += s * s
            return total / (get(slice(LEAVES * K, LEAVES * K + LEAVES)) + ridge)

        gain = (
            squares(lambda r: side_sums(0, r))
            + squares(lambda r: side_sums(1, r))
            - squares(lambda r: side_sums(0, r) + side_sums(1, r))
        )
        lane = lax.broadcasted_iota(jnp.int32, (1, cols), 1)
        counts = jnp.zeros((1, cols), jnp.int32)
        fetches[5].wait()
        for f in range(GROUP):
            counts = jnp.where(lane // BINS == f, nbins_ref[z * GROUP + f], counts)
        gain = jnp.where(lane % BINS < counts - 1, gain, 0.0)
        for i in range(NZ):
            gain_s[i] = gain[i * LP : (i + 1) * LP]

    def gain_copy(t):
        other = (z + far_first(t, NZ)) % NZ
        return remote(gain_s.at[other], gain_r.at[z], gs_sem.at[t], gr_sem.at[z], dev(x, y, other, c))

    pair = remote(pair_s, pair_r, pair_sem.at[0], pair_sem.at[1], dev(x, y, z, 1 - c))
    plane = [(i, j) for i in range(NX) for j in range(NY) if i or j]
    plane.sort(key=lambda step: -min(step[0], NX - step[0]) - min(step[1], NY - step[1]))
    here = x * NY + y

    def best_copy(t):
        i, j = plane[t]
        device = dev((x + i) % NX, (y + j) % NY, z, c)
        return remote(best_s, best_r.at[here], bs_sem.at[t], br_sem.at[here], device)

    with jax.named_scope("column"):

        @pl.loop(0, NZ - 1)
        def _(t):
            gain_copy(t).start()

        gain_r[z] = gain_s[z]

        @pl.loop(1, NZ)
        def _(i):
            other = (z + i) % NZ
            remote(gain_s.at[0], gain_r.at[other], gs_sem.at[0], gr_sem.at[other], dev(x, y, z, c)).wait_recv()

        best = jnp.max(functools.reduce(jnp.maximum, [gain_r[i] for i in range(NZ)]), axis=1, keepdims=True)
        pair_s[...] = jnp.broadcast_to(best, (LP, LANES))

    with jax.named_scope("pair"):
        pair.start()
        pair.wait_recv()
        best_s[...] = jnp.maximum(pair_s[...], pair_r[...])

    with jax.named_scope("plane"):
        for t in range(NX * NY - 1):
            best_copy(t).start()
        best_r[here] = best_s[...]

        @pl.loop(1, NX * NY)
        def _(i):
            other = (here + i) % (NX * NY)
            remote(best_s, best_r.at[other], bs_sem.at[0], br_sem.at[other], dev(x, y, z, c)).wait_recv()

        best = functools.reduce(jnp.maximum, [best_r[i] for i in range(NX * NY)])[:, :1]
        for i in range(NZ):
            out_ref[:, i * cols : (i + 1) * cols] = gain_r[i] / (best + epsilon)

    with jax.named_scope("sends"):

        @pl.loop(0, NZ)
        def _(i):
            column_values(i, "wait")
            column_bins(i, "wait")

        @pl.loop(0, NY - 1)
        def _(t):
            for copy in y_copies(t):
                copy.wait_send()

        @pl.loop(0, NY)
        def _(ys):
            @pl.loop(0, NX - 1)
            def _(t):
                for copy in x_copies(t, ys):
                    copy.wait_send()

        swap.wait_send()
        pair.wait_send()

        @pl.loop(0, NZ - 1)
        def _(t):
            gain_copy(t).wait_send()

        for t in range(NX * NY - 1):
            best_copy(t).wait_send()


def on_device(NX, NY, NZ, logits, labels, projection, bins, nbins, leaf):
    bf16, f32 = jnp.bfloat16, jnp.float32
    HZ = NZ // 2
    LP = LEAVES // NZ
    rows, classes = logits.shape
    span = HZ * LANES
    cols = GROUP * BINS
    tall = LEAVES * (K + 1)
    VMEM, DMA = pltpu.VMEM, pltpu.SemaphoreType.DMA
    vmem = pl.BlockSpec(memory_space=pltpu.VMEM)
    hbm = pl.BlockSpec(memory_space=pl.ANY)
    half = NX * NY // 2
    bin_block = (GROUP * NX, NY * LANES)
    return pl.pallas_call(
        functools.partial(kernel, NX, NY, NZ),
        out_shape=jax.ShapeDtypeStruct((LP, NZ * cols), f32),
        in_specs=[hbm] * 6,
        out_specs=vmem,
        scratch_shapes=[
            VMEM(logits.shape, bf16),
            VMEM((1, rows), jnp.int32),
            VMEM((K, classes), bf16),
            VMEM(bins.shape, jnp.int32),
            pltpu.SMEM(nbins.shape, jnp.int32),
            VMEM((2 * half, LANES), jnp.int32),
            VMEM((2 * rows, classes), bf16),
            VMEM((NZ, *bin_block), bf16),
            VMEM((half, LANES), bf16),
            VMEM((K, LANES), bf16),
            VMEM((1, LANES), f32),
            VMEM((NZ, *bin_block), bf16),
            VMEM((NZ, half, LANES), bf16),
            VMEM((NZ, K, LANES), bf16),
            VMEM((NZ, 1, LANES), f32),
            VMEM((NZ, NY, GROUP * NX, LANES), f32),
            VMEM((HZ, 2 * half, LANES), f32),
            VMEM((NX, NY, K, span), bf16),
            VMEM((NX, NY, 1, span), f32),
            VMEM((tall, QUAD * span), bf16),
            VMEM((2, cols, QUAD * span), bf16),
            VMEM((2, tall, cols), f32),
            VMEM((tall, cols), f32),
            VMEM((2, cols // LANES, tall, LANES), f32),
            VMEM((NZ, LP, cols), f32),
            VMEM((NZ, LP, cols), f32),
            VMEM((LP, LANES), f32),
            VMEM((LP, LANES), f32),
            VMEM((LP, LANES), f32),
            VMEM((NX * NY, LP, LANES), f32),
            DMA((6,)),
            DMA((4, NZ)),
            DMA((4, NZ)),
            DMA((2, NY)),
            DMA((NY, 2)),
            DMA((NX, 2, NY)),
            DMA((NX, NY, 2)),
            DMA((2,)),
            DMA((NZ,)),
            DMA((NZ,)),
            DMA((2,)),
            DMA((NX * NY,)),
            DMA((NX * NY,)),
        ],
        compiler_params=pltpu.CompilerParams(
            collective_id=0, has_side_effects=True, vmem_limit_bytes=62 * 2**20
        ),
        cost_estimate=pl.CostEstimate(
            flops=2 * tall * 2 * cols * NX * NY * span, bytes_accessed=2**20, transcendentals=rows * classes
        ),
    )(
        logits,
        labels.reshape(1, rows),
        projection.T,
        bins,
        nbins,
        leaf.reshape(2 * half, LANES),
    )


def solution(mesh, NX=4, NY=8):
    return jax.shard_map(
        functools.partial(on_device, NX, NY, mesh.shape["row"]),
        mesh=mesh,
        in_specs=(
            P(("row", "feat"), None),
            P(("row", "feat")),
            P(),
            P("feat", "row"),
            P("feat"),
            P("row"),
        ),
        out_specs=P("row", "feat"),
        check_vma=False,
    )
```

time: 63.2 us -> 54 us (0.85)
  Pallas kernels: 58.2 us -> 52.5 us
  local copies, waits for them, and re-layouts: 4.7 us -> 1.32 us
    pallas_call x1, Pallas kernels: 58.2 us -> 52.5 us  [on_device(): pl.pallas_call(functools.partial(kernel, NX, NY, NZ), out_shape=jax.Shape...]
    unnamed x13 -> x1, local copies, waits for them, and re-layouts: 4.7 us -> 1.32 us
where the time goes in v2:
time: 54 us; the launch traced here: 53.8 us
  Pallas kernels  52.5 us (97%)
  local copies, waits for them, and re-layouts  1.32 us (2%)
    pallas_call x1, Pallas kernels, on_device(): pl.pallas_call(functools.partial(kernel, NX, NY, NZ), out_shape=jax.Shape...  52.5 us
    unnamed x1, local copies, waits for them, and re-layouts  1.32 us

profile of v2, /device:TPU:1, one launch (start us, length us, event | category | flops | bytes accessed | tf_op | source)
XLA Modules:
  0.0 53.8 jit_solution(9335892814794464133)
XLA Ops:
  0.0 52.5 %shard_map.64 = f32[2,2048]{1,0:T(2,128)} custom-call(bf16[64,1000]{1,0:T(8,128)(2,1)} %logits_any.1, s32[1,64]{1,0:T(1,128)} %bitcast.5, bf16[16,1000]{1,0:T(8,128)(2,1)} %bitcast.3, s32[32,4096]{1,0:T(8,128)} %bins_any.1, s32[32]{0:T(128)} %nbins_any.1, s32[32,128]{1,0:T(8,128)} %bitcast.4), custom_call_target="tpu_custom_call" | custom-call | flops 4563402752 | bytes 1048576 | tf_op jit(solution)/shard_map/pallas_call | solution.py:475
  52.5 1.3 %copy.8 = f32[2,2048]{1,0:T(2,128)} copy(f32[2,2048]{1,0:T(2,128)} %shard_map.64) | data formatting | bytes 32768

commit v3 on v2

--- a/solution.py
+++ b/solution.py
@@ -47,17 +47,12 @@
     leaf_ref,
     grad,
     bins_s,
-    leaf_s,
-    zsk_s,
-    zhs_s,
+    rows_s,
     bins_r,
-    leaf_r,
-    zsk_r,
-    zhs_r,
+    rows_r,
     bins_f,
     leaf_f,
-    sk,
-    hs,
+    vals,
     weights,
     onehot,
     acc,
@@ -70,18 +65,14 @@
     best_s,
     best_r,
     local_sem,
-    zs_sem,
-    zr_sem,
-    ys_sem,
-    yr_sem,
-    xs_sem,
-    xr_sem,
-    hist_sem,
-    gs_sem,
-    gr_sem,
+    column_sem,
+    send_sem,
+    y_sem,
+    x_sem,
+    swap_sem,
+    gain_sem,
     pair_sem,
-    bs_sem,
-    br_sem,
+    best_sem,
 ):
     HZ = NZ // 2
     LP = LEAVES // NZ
@@ -148,104 +139,94 @@
         grad[...] = jnp.zeros_like(grad)
         grad[pl.ds(pl.multiple_of(c * rows, rows), rows), :] = gradient.astype(jnp.bfloat16)
         sketch = lax.dot_general(proj_ref[...], grad[...], NT, preferred_element_type=jnp.float32)
-        zsk_s[...] = sketch.astype(jnp.bfloat16)
+        rows_s[:, :LANES] = sketch.astype(jnp.bfloat16)
         hessian = jnp.sum(probability * (1.0 - probability), axis=1, keepdims=True)
-        hessian = hessian.astype(jnp.bfloat16).astype(jnp.float32)
         lane = lax.broadcasted_iota(jnp.int32, (rows, LANES), 1)
         line = lax.broadcasted_iota(jnp.int32, (rows, LANES), 0)
-        zhs_s[...] = jnp.sum(jnp.where(lane == line + c * rows, hessian, 0.0), axis=0, keepdims=True)
+        hessian = jnp.sum(jnp.where(lane == line + c * rows, hessian, 0.0), axis=0, keepdims=True)
+        rows_s[:, LANES:] = jnp.broadcast_to(hessian, (K, LANES)).astype(jnp.bfloat16)
+
+    with jax.named_scope("regroup"):
+        fetches[0].wait()
+        fetches[4].wait()
+        width = NY * LANES
+        half = NX * NY // 2
+        leaf = leaf_ref[pl.ds(pl.multiple_of(c * half, half), half), :].astype(jnp.float32).astype(jnp.bfloat16)
+        for d in range(NZ):
+            four = bins_v[d * GROUP : (d + 1) * GROUP, :].astype(jnp.float32)
+            bins_s[d, :, :width] = jnp.concatenate(
+                [four[:, i * width : (i + 1) * width] for i in range(NX)], axis=0
+            ).astype(jnp.bfloat16)
+            bins_s[d, :half, width:] = leaf
 
     with jax.named_scope("barrier"):
         pl.semaphore_wait(barrier, 2 * NZ - 1 + NY - 1 + NX - 1)
 
     def to_column(t, src, dst, kind, act):
         device = dev(x, y, (z + far_first(t, NZ)) % NZ, h)
-        send, recv = zs_sem.at[kind, t], zr_sem.at[kind, slot]
         here = (t == NZ - 1) & (c == h)
 
         @pl.when(here)
         def _():
             if act == "start":
-                pltpu.make_async_copy(src, dst, recv).start()
+                pltpu.make_async_copy(src, dst, column_sem.at[kind]).start()
 
         @pl.when(jnp.logical_not(here))
         def _():
-            copy = remote(src, dst, send, recv, device)
+            copy = remote(src, dst, send_sem.at[kind], column_sem.at[kind], device)
             if act == "start":
                 copy.start()
             else:
                 copy.wait_send()
 
-    def column_values(i, act):
-        to_column(i, zsk_s, zsk_r.at[slot], 0, act)
-        to_column(i, zhs_s, zhs_r.at[slot], 1, act)
-
-    def column_bins(i, act):
-        to_column(i, bins_s.at[(z + far_first(i, NZ)) % NZ], bins_r.at[slot], 2, act)
-        to_column(i, leaf_s, leaf_r.at[slot], 3, act)
+    def column_values(t, act):
+        to_column(t, rows_s, rows_r.at[slot], 0, act)
+
+    def column_bins(t, act):
+        to_column(t, bins_s.at[(z + far_first(t, NZ)) % NZ], bins_r.at[slot], 1, act)
 
     @pl.loop(0, NZ)
-    def _(i):
-        column_values(i, "start")
-
-    with jax.named_scope("regroup"):
-        fetches[0].wait()
-        fetches[4].wait()
-        width = NY * LANES
-        for d in range(NZ):
-            four = bins_v[d * GROUP : (d + 1) * GROUP, :].astype(jnp.float32)
-            bins_s[d] = jnp.concatenate(
-                [four[:, i * width : (i + 1) * width] for i in range(NX)], axis=0
-            ).astype(jnp.bfloat16)
-        half = NX * NY // 2
-        leaf_s[...] = leaf_ref[pl.ds(pl.multiple_of(c * half, half), half), :].astype(jnp.float32).astype(jnp.bfloat16)
+    def _(t):
+        column_values(t, "start")
 
     @pl.loop(0, NZ)
-    def _(i):
-        column_bins(i, "start")
-
-    def block_copies(step, xs, ys, device, send, recv):
-        return (
-            remote(sk.at[xs, ys], sk.at[xs, ys], send.at[0, step], recv.at[0], device),
-            remote(hs.at[xs, ys], hs.at[xs, ys], send.at[1, step], recv.at[1], device),
-        )
+    def _(t):
+        column_bins(t, "start")
+
+    def await_bytes(ref, sem):
+        pltpu.make_async_copy(ref, ref, sem).wait()
 
     with jax.named_scope("zvalues"):
-        lane = lax.broadcasted_iota(jnp.int32, (1, LANES), 1)
-        first = lane < rows
-
-        @pl.loop(0, 2 * HZ)
-        def _(i):
-            remote(zsk_s, zsk_r.at[i], zs_sem.at[0, 0], zr_sem.at[0, i], dev(x, y, z, c)).wait_recv()
-            remote(zhs_s, zhs_r.at[i], zs_sem.at[0, 0], zr_sem.at[1, i], dev(x, y, z, c)).wait_recv()
-
+        await_bytes(rows_r, column_sem.at[0])
+        first = lax.broadcasted_iota(jnp.int32, (1, LANES), 1) < rows
+        line = lax.broadcasted_iota(jnp.int32, (K, LANES), 0)
+        hessians = jnp.zeros((K, LANES), jnp.float32)
         for i in range(HZ):
-            span = slice(i * LANES, (i + 1) * LANES)
-            sk[x, y, :, span] = jnp.where(
-                first, zsk_r[2 * i].astype(jnp.float32), zsk_r[2 * i + 1].astype(jnp.float32)
-            ).astype(jnp.bfloat16)
-            hs[x, y, :, span] = jnp.where(first, zhs_r[2 * i], zhs_r[2 * i + 1])
-
-    def y_copies(t):
+            both = [rows_r[2 * i + j].astype(jnp.float32) for j in range(2)]
+            merged = jnp.where(first, both[0][:, :LANES], both[1][:, :LANES])
+            vals[x, y, :, i * LANES : (i + 1) * LANES] = merged.astype(jnp.bfloat16)
+            merged = jnp.where(first, both[0][:, LANES:], both[1][:, LANES:])
+            hessians = jnp.where(line == i, merged, hessians)
+        vals[x, y, :, HZ * LANES :] = hessians.astype(jnp.bfloat16)
+
+    def y_copy(t):
         device = dev(x, (y + far_first(t, NY)) % NY, z, c)
-        return block_copies(t, x, y, device, ys_sem, yr_sem.at[y])
-
-    def x_copies(t, ys):
+        return remote(vals.at[x, y], vals.at[x, y], send_sem.at[2], y_sem.at[y], device)
+
+    def x_copy(t, ys, quad):
         device = dev((x + far_first(t, NX)) % NX, y, z, c)
-        return block_copies(ys, x, ys, device, xs_sem.at[t], xr_sem.at[x, ys])
-
-    def forward(ys):
+        return remote(vals.at[x, ys], vals.at[x, ys], send_sem.at[3], x_sem.at[x, quad], device)
+
+    def forward(ys, quad):
         @pl.loop(0, NX - 1)
         def _(t):
-            for copy in x_copies(t, ys):
-                copy.start()
+            x_copy(t, ys, quad).start()
 
     @pl.loop(0, NY - 1)
     def _(t):
-        for copy in y_copies(t):
-            copy.start()
-
-    forward(y)
+        y_copy(t).start()
+
+    forward(y, 0)
     acc[...] = jnp.zeros_like(acc)
 
     def near_y(t):
@@ -253,19 +234,17 @@
 
     def await_y(t):
         ys = near_y(t)
-        for copy in block_copies(0, x, ys, dev(x, y, z, c), ys_sem, yr_sem.at[ys]):
-            copy.wait_recv()
-        forward(ys)
+        await_bytes(vals.at[x, ys], y_sem.at[ys])
+        forward(ys, t // QUAD)
 
     pl.loop(1, QUAD)(await_y)
 
     with jax.named_scope("zbins"):
+        await_bytes(bins_r, column_sem.at[1])
         for i in range(2 * HZ):
-            remote(bins_s.at[0], bins_r.at[i], zs_sem.at[0, 0], zr_sem.at[2, i], dev(x, y, z, c)).wait_recv()
-            remote(leaf_s, leaf_r.at[i], zs_sem.at[0, 0], zr_sem.at[3, i], dev(x, y, z, c)).wait_recv()
             for j in range(NY):
                 bins_f[i, j] = bins_r[i, :, j * LANES : (j + 1) * LANES].astype(jnp.float32)
-            leaf_f[i // 2, (i % 2) * half : (i % 2 + 1) * half] = leaf_r[i].astype(jnp.float32)
+            leaf_f[i // 2, (i % 2) * half : (i % 2 + 1) * half] = bins_r[i, :half, width:].astype(jnp.float32)
 
     bin_ids = lax.broadcasted_iota(jnp.int32, (BINS, LANES), 0).astype(jnp.float32).astype(jnp.bfloat16)
     leaf_ids = lax.broadcasted_iota(jnp.int32, (LEAVES, LANES), 0).astype(jnp.float32).astype(jnp.bfloat16)
@@ -274,15 +253,16 @@
     def build(xs, quad):
         for b in range(QUAD):
             ys = near_y(quad * QUAD + b)
+            hessians = vals[xs, ys, :, HZ * LANES :].astype(jnp.float32)
             for i in range(HZ):
                 src = slice(i * LANES, (i + 1) * LANES)
                 dst = slice((b * HZ + i) * LANES, (b * HZ + i + 1) * LANES)
                 leaf = leaf_f[i, pl.ds(xs * NY + ys, 1), :]
                 leaf = jnp.broadcast_to(leaf, (LEAVES, LANES)).astype(jnp.bfloat16)
-                tile = sk[xs, ys, :, src]
+                tile = vals[xs, ys, :, src]
                 for l in range(LEAVES):
                     weights[l * K : (l + 1) * K, dst] = jnp.where(leaf == jnp.bfloat16(l), tile, nil)
-                hess = jnp.broadcast_to(hs[xs, ys, :, src], (LEAVES, LANES)).astype(jnp.bfloat16)
+                hess = jnp.broadcast_to(hessians[i : i + 1], (LEAVES, LANES)).astype(jnp.bfloat16)
                 weights[LEAVES * K :, dst] = jnp.where(leaf == leaf_ids, hess, nil)
                 for side in range(2):
                     for f in range(GROUP):
@@ -311,15 +291,10 @@
     def await_x(t):
         quad, xs = t // (NX - 1), (x + near_first(t % (NX - 1) + 1) + NX) % NX
 
-        @pl.loop(quad * QUAD, (quad + 1) * QUAD)
-        def _(i):
-            ys = near_y(i)
-            for copy in block_copies(0, xs, ys, dev(x, y, z, c), xs_sem.at[0], xr_sem.at[xs, ys]):
-                copy.wait_recv()
-
+        await_bytes(vals.at[xs, pl.ds(0, QUAD)], x_sem.at[xs, quad])
         return xs, quad
 
-    swap = remote(acc.at[1 - c], hist_r, hist_sem.at[0], hist_sem.at[1], dev(x, y, z, 1 - c))
+    swap = remote(acc.at[1 - c], hist_r, swap_sem.at[0], swap_sem.at[1], dev(x, y, z, 1 - c))
     n_quads = (NX - 1) * (NY // QUAD)
 
     with jax.named_scope("slabs"):
@@ -382,7 +357,7 @@
 
     def gain_copy(t):
         other = (z + far_first(t, NZ)) % NZ
-        return remote(gain_s.at[other], gain_r.at[z], gs_sem.at[t], gr_sem.at[z], dev(x, y, other, c))
+        return remote(gain_s.at[other], gain_r.at[z], gain_sem.at[0], gain_sem.at[1], dev(x, y, other, c))
 
     pair = remote(pair_s, pair_r, pair_sem.at[0], pair_sem.at[1], dev(x, y, z, 1 - c))
     plane = [(i, j) for i in range(NX) for j in range(NY) if i or j]
@@ -392,7 +367,7 @@
     def best_copy(t):
         i, j = plane[t]
         device = dev((x + i) % NX, (y + j) % NY, z, c)
-        return remote(best_s, best_r.at[here], bs_sem.at[t], br_sem.at[here], device)
+        return remote(best_s, best_r.at[here], best_sem.at[0], best_sem.at[1], device)
 
     with jax.named_scope("column"):
 
@@ -402,11 +377,7 @@
 
         gain_r[z] = gain_s[z]
 
-        @pl.loop(1, NZ)
-        def _(i):
-            other = (z + i) % NZ
-            remote(gain_s.at[0], gain_r.at[other], gs_sem.at[0], gr_sem.at[other], dev(x, y, z, c)).wait_recv()
-
+        await_bytes(gain_r.at[pl.ds(0, NZ - 1)], gain_sem.at[1])
         best = jnp.max(functools.reduce(jnp.maximum, [gain_r[i] for i in range(NZ)]), axis=1, keepdims=True)
         pair_s[...] = jnp.broadcast_to(best, (LP, LANES))
 
@@ -420,11 +391,7 @@
             best_copy(t).start()
         best_r[here] = best_s[...]
 
-        @pl.loop(1, NX * NY)
-        def _(i):
-            other = (here + i) % (NX * NY)
-            remote(best_s, best_r.at[other], bs_sem.at[0], br_sem.at[other], dev(x, y, z, c)).wait_recv()
-
+        await_bytes(best_r.at[pl.ds(0, NX * NY - 1)], best_sem.at[1])
         best = functools.reduce(jnp.maximum, [best_r[i] for i in range(NX * NY)])[:, :1]
         for i in range(NZ):
             out_ref[:, i * cols : (i + 1) * cols] = gain_r[i] / (best + epsilon)
@@ -432,31 +399,16 @@
     with jax.named_scope("sends"):
 
         @pl.loop(0, NZ)
-        def _(i):
-            column_values(i, "wait")
-            column_bins(i, "wait")
-
-        @pl.loop(0, NY - 1)
         def _(t):
-            for copy in y_copies(t):
-                copy.wait_send()
-
-        @pl.loop(0, NY)
-        def _(ys):
-            @pl.loop(0, NX - 1)
-            def _(t):
-                for copy in x_copies(t, ys):
-                    copy.wait_send()
-
+            column_values(t, "wait")
+            column_bins(t, "wait")
+
+        await_bytes(vals.at[0, pl.ds(0, NY - 1)], send_sem.at[2])
+        await_bytes(vals.at[pl.ds(0, NX - 1)], send_sem.at[3])
         swap.wait_send()
         pair.wait_send()
-
-        @pl.loop(0, NZ - 1)
-        def _(t):
-            gain_copy(t).wait_send()
-
-        for t in range(NX * NY - 1):
-            best_copy(t).wait_send()
+        await_bytes(gain_s.at[pl.ds(0, NZ - 1)], gain_sem.at[0])
+        await_bytes(best_r.at[pl.ds(0, NX * NY - 1)], best_sem.at[0])
 
 
 def on_device(NX, NY, NZ, logits, labels, projection, bins, nbins, leaf):
@@ -471,7 +423,7 @@
     vmem = pl.BlockSpec(memory_space=pltpu.VMEM)
     hbm = pl.BlockSpec(memory_space=pl.ANY)
     half = NX * NY // 2
-    bin_block = (GROUP * NX, NY * LANES)
+    bin_block = (GROUP * NX, (NY + 1) * LANES)
     return pl.pallas_call(
         functools.partial(kernel, NX, NY, NZ),
         out_shape=jax.ShapeDtypeStruct((LP, NZ * cols), f32),
@@ -486,17 +438,12 @@
             VMEM((2 * half, LANES), jnp.int32),
             VMEM((2 * rows, classes), bf16),
             VMEM((NZ, *bin_block), bf16),
-            VMEM((half, LANES), bf16),
-            VMEM((K, LANES), bf16),
-            VMEM((1, LANES), f32),
+            VMEM((K, 2 * LANES), bf16),
             VMEM((NZ, *bin_block), bf16),
-            VMEM((NZ, half, LANES), bf16),
-            VMEM((NZ, K, LANES), bf16),
-            VMEM((NZ, 1, LANES), f32),
+            VMEM((NZ, K, 2 * LANES), bf16),
             VMEM((NZ, NY, GROUP * NX, LANES), f32),
             VMEM((HZ, 2 * half, LANES), f32),
-            VMEM((NX, NY, K, span), bf16),
-            VMEM((NX, NY, 1, span), f32),
+            VMEM((NX, NY, K, span + LANES), bf16),
             VMEM((tall, QUAD * span), bf16),
             VMEM((2, cols, QUAD * span), bf16),
             VMEM((2, tall, cols), f32),
@@ -509,18 +456,14 @@
             VMEM((LP, LANES), f32),
             VMEM((NX * NY, LP, LANES), f32),
             DMA((6,)),
-            DMA((4, NZ)),
-            DMA((4, NZ)),
-            DMA((2, NY)),
-            DMA((NY, 2)),
-            DMA((NX, 2, NY)),
-            DMA((NX, NY, 2)),
             DMA((2,)),
-            DMA((NZ,)),
-            DMA((NZ,)),
+            DMA((4,)),
+            DMA((NY,)),
+            DMA((NX, NY // QUAD)),
             DMA((2,)),
-            DMA((NX * NY,)),
-            DMA((NX * NY,)),
+            DMA((2,)),
+            DMA((2,)),
+            DMA((2,)),
         ],
         compiler_params=pltpu.CompilerParams(
             collective_id=0, has_side_effects=True, vmem_limit_bytes=62 * 2**20

time: 54 us -> 51.3 us (0.950)
  Pallas kernels: 52.5 us -> 49.7 us
    pallas_call x1, Pallas kernels: 52.5 us -> 49.7 us  [on_device(): pl.pallas_call(functools.partial(kernel, NX, NY, NZ), out_shape=jax.Shape...]
where the time goes in v3:
time: 51.3 us; the launch traced here: 51.1 us
  Pallas kernels  49.7 us (97%)
  local copies, waits for them, and re-layouts  1.32 us (3%)
    pallas_call x1, Pallas kernels, on_device(): pl.pallas_call(functools.partial(kernel, NX, NY, NZ), out_shape=jax.Shape...  49.7 us
    unnamed x1, local copies, waits for them, and re-layouts  1.32 us

profile of v3, /device:TPU:1, one launch (start us, length us, event | category | flops | bytes accessed | tf_op | source)
XLA Modules:
  0.0 51.1 jit_solution(13484294669969465466)
XLA Ops:
  0.0 49.7 %shard_map.64 = f32[2,2048]{1,0:T(2,128)} custom-call(bf16[64,1000]{1,0:T(8,128)(2,1)} %logits_any.1, s32[1,64]{1,0:T(1,128)} %bitcast.5, bf16[16,1000]{1,0:T(8,128)(2,1)} %bitcast.3, s32[32,4096]{1,0:T(8,128)} %bins_any.1, s32[32]{0:T(128)} %nbins_any.1, s32[32,128]{1,0:T(8,128)} %bitcast.4), custom_call_target="tpu_custom_call" | custom-call | flops 4563402752 | bytes 1048576 | tf_op jit(solution)/shard_map/pallas_call | solution.py:427
  49.8 1.3 %copy.8 = f32[2,2048]{1,0:T(2,128)} copy(f32[2,2048]{1,0:T(2,128)} %shard_map.64) | data formatting | bytes 32768

commit v4 on v3

--- a/solution.py
+++ b/solution.py
@@ -51,7 +51,6 @@
     bins_r,
     rows_r,
     bins_f,
-    leaf_f,
     vals,
     weights,
     onehot,
@@ -60,8 +59,8 @@
     sums,
     gain_s,
     gain_r,
-    pair_s,
-    pair_r,
+    peak_s,
+    peak_r,
     best_s,
     best_r,
     local_sem,
@@ -71,7 +70,7 @@
     x_sem,
     swap_sem,
     gain_sem,
-    pair_sem,
+    peak_sem,
     best_sem,
 ):
     HZ = NZ // 2
@@ -110,21 +109,19 @@
     def greet(device):
         pl.semaphore_signal(barrier, inc=1, device_id=device, device_id_type=MESH)
 
-    @pl.loop(1, 2 * NZ)
-    def _(i):
-        other = (z * 2 + c + i) % (2 * NZ)
-        greet(dev(x, y, other // 2, other % 2))
-
-    @pl.loop(1, NY)
-    def _(i):
-        greet(dev(x, (y + i) % NY, z, c))
-
-    @pl.loop(1, NX)
-    def _(i):
-        greet(dev((x + i) % NX, y, z, c))
+    for t in range(max(NX, NY, NZ)):
+        if t < NZ:
+            other = (z + far_first(t, NZ)) % NZ
+            greet(dev(x, y, other, 1 - c))
+            if t < NZ - 1:
+                greet(dev(x, y, other, c))
+        if t < NY - 1:
+            greet(dev(x, (y + far_first(t, NY)) % NY, z, c))
+        if t < NX - 1:
+            greet(dev((x + far_first(t, NX)) % NX, y, z, c))
 
     with jax.named_scope("softmax"):
-        for fetch in fetches[1:4]:
+        for fetch in fetches[1:5]:
             fetch.wait()
         lane = lax.broadcasted_iota(jnp.int32, (rows, rows), 1)
         line = lax.broadcasted_iota(jnp.int32, (rows, rows), 0)
@@ -139,25 +136,24 @@
         grad[...] = jnp.zeros_like(grad)
         grad[pl.ds(pl.multiple_of(c * rows, rows), rows), :] = gradient.astype(jnp.bfloat16)
         sketch = lax.dot_general(proj_ref[...], grad[...], NT, preferred_element_type=jnp.float32)
-        rows_s[:, :LANES] = sketch.astype(jnp.bfloat16)
         hessian = jnp.sum(probability * (1.0 - probability), axis=1, keepdims=True)
         lane = lax.broadcasted_iota(jnp.int32, (rows, LANES), 1)
         line = lax.broadcasted_iota(jnp.int32, (rows, LANES), 0)
-        hessian = jnp.sum(jnp.where(lane == line + c * rows, hessian, 0.0), axis=0, keepdims=True)
-        rows_s[:, LANES:] = jnp.broadcast_to(hessian, (K, LANES)).astype(jnp.bfloat16)
+        hessian = jnp.sum(jnp.where(lane == line + (1 - c) * rows, hessian, 0.0), axis=0, keepdims=True)
+        leaf = pltpu.roll(leaf_ref[pl.ds(x * NY + y, 1), :].astype(jnp.float32), rows, 1)
+        lane = lax.broadcasted_iota(jnp.int32, (K, LANES), 1)
+        line = lax.broadcasted_iota(jnp.int32, (K, LANES), 0)
+        beside = jnp.where(line == 0, hessian, jnp.where(line == 1, leaf, 0.0))
+        rows_s[...] = jnp.where(lane // rows == c, sketch, beside).astype(jnp.bfloat16)
 
     with jax.named_scope("regroup"):
         fetches[0].wait()
-        fetches[4].wait()
         width = NY * LANES
-        half = NX * NY // 2
-        leaf = leaf_ref[pl.ds(pl.multiple_of(c * half, half), half), :].astype(jnp.float32).astype(jnp.bfloat16)
         for d in range(NZ):
             four = bins_v[d * GROUP : (d + 1) * GROUP, :].astype(jnp.float32)
-            bins_s[d, :, :width] = jnp.concatenate(
+            bins_s[d] = jnp.concatenate(
                 [four[:, i * width : (i + 1) * width] for i in range(NX)], axis=0
             ).astype(jnp.bfloat16)
-            bins_s[d, :half, width:] = leaf
 
     with jax.named_scope("barrier"):
         pl.semaphore_wait(barrier, 2 * NZ - 1 + NY - 1 + NX - 1)
@@ -200,14 +196,13 @@
         await_bytes(rows_r, column_sem.at[0])
         first = lax.broadcasted_iota(jnp.int32, (1, LANES), 1) < rows
         line = lax.broadcasted_iota(jnp.int32, (K, LANES), 0)
-        hessians = jnp.zeros((K, LANES), jnp.float32)
+        beside = jnp.zeros((K, LANES), jnp.float32)
         for i in range(HZ):
-            both = [rows_r[2 * i + j].astype(jnp.float32) for j in range(2)]
-            merged = jnp.where(first, both[0][:, :LANES], both[1][:, :LANES])
-            vals[x, y, :, i * LANES : (i + 1) * LANES] = merged.astype(jnp.bfloat16)
-            merged = jnp.where(first, both[0][:, LANES:], both[1][:, LANES:])
-            hessians = jnp.where(line == i, merged, hessians)
-        vals[x, y, :, HZ * LANES :] = hessians.astype(jnp.bfloat16)
+            low, high = rows_r[2 * i].astype(jnp.float32), rows_r[2 * i + 1].astype(jnp.float32)
+            vals[x, y, :, i * LANES : (i + 1) * LANES] = jnp.where(first, low, high).astype(jnp.bfloat16)
+            other = pltpu.roll(jnp.where(first, high, low), rows, 1)
+            beside = jnp.where(line == i, other[0:1], jnp.where(line == HZ + i, other[1:2], beside))
+        vals[x, y, :, HZ * LANES :] = beside.astype(jnp.bfloat16)
 
     def y_copy(t):
         device = dev(x, (y + far_first(t, NY)) % NY, z, c)
@@ -237,32 +232,31 @@
         await_bytes(vals.at[x, ys], y_sem.at[ys])
         forward(ys, t // QUAD)
 
-    pl.loop(1, QUAD)(await_y)
+    pl.loop(1, NY)(await_y)
 
     with jax.named_scope("zbins"):
         await_bytes(bins_r, column_sem.at[1])
         for i in range(2 * HZ):
             for j in range(NY):
                 bins_f[i, j] = bins_r[i, :, j * LANES : (j + 1) * LANES].astype(jnp.float32)
-            leaf_f[i // 2, (i % 2) * half : (i % 2 + 1) * half] = bins_r[i, :half, width:].astype(jnp.float32)
 
     bin_ids = lax.broadcasted_iota(jnp.int32, (BINS, LANES), 0).astype(jnp.float32).astype(jnp.bfloat16)
     leaf_ids = lax.broadcasted_iota(jnp.int32, (LEAVES, LANES), 0).astype(jnp.float32).astype(jnp.bfloat16)
     one, nil = jnp.bfloat16(1), jnp.bfloat16(0)
 
-    def build(xs, quad):
+    def build(part, xs, quad):
         for b in range(QUAD):
             ys = near_y(quad * QUAD + b)
-            hessians = vals[xs, ys, :, HZ * LANES :].astype(jnp.float32)
+            beside = vals[xs, ys, :, HZ * LANES :].astype(jnp.float32)
             for i in range(HZ):
                 src = slice(i * LANES, (i + 1) * LANES)
-                dst = slice((b * HZ + i) * LANES, (b * HZ + i + 1) * LANES)
-                leaf = leaf_f[i, pl.ds(xs * NY + ys, 1), :]
-                leaf = jnp.broadcast_to(leaf, (LEAVES, LANES)).astype(jnp.bfloat16)
+                at = ((part * QUAD + b) * HZ + i) * LANES
+                dst = slice(at, at + LANES)
+                hess = jnp.broadcast_to(beside[i : i + 1], (LEAVES, LANES)).astype(jnp.bfloat16)
+                leaf = jnp.broadcast_to(beside[HZ + i : HZ + i + 1], (LEAVES, LANES)).astype(jnp.bfloat16)
                 tile = vals[xs, ys, :, src]
                 for l in range(LEAVES):
                     weights[l * K : (l + 1) * K, dst] = jnp.where(leaf == jnp.bfloat16(l), tile, nil)
-                hess = jnp.broadcast_to(hessians[i : i + 1], (LEAVES, LANES)).astype(jnp.bfloat16)
                 weights[LEAVES * K :, dst] = jnp.where(leaf == leaf_ids, hess, nil)
                 for side in range(2):
                     for f in range(GROUP):
@@ -270,23 +264,18 @@
                         ids = jnp.broadcast_to(ids, (BINS, LANES)).astype(jnp.bfloat16)
                         onehot[side, f * BINS : (f + 1) * BINS, dst] = jnp.where(ids == bin_ids, one, nil)
 
-    def add_side(side):
-        acc[side] += lax.dot_general(weights[...], onehot[side], NT, preferred_element_type=jnp.float32)
-
-    def add_quad(xs, quad):
-        build(xs, quad)
-        add_side(0)
-        add_side(1)
+    def add_side(parts, side):
+        depth = slice(0, parts * QUAD * HZ * LANES)
+        acc[side] += lax.dot_general(weights[:, depth], onehot[side, :, depth], NT, preferred_element_type=jnp.float32)
+
+    def add_both(parts):
+        add_side(parts, 0)
+        add_side(parts, 1)
 
     with jax.named_scope("ownslab"):
-
-        @pl.loop(0, NY // QUAD)
-        def _(quad):
-            @pl.when(quad > 0)
-            def _():
-                pl.loop(quad * QUAD, (quad + 1) * QUAD)(await_y)
-
-            add_quad(x, quad)
+        for quad in range(NY // QUAD):
+            build(quad, x, quad)
+        add_both(NY // QUAD)
 
     def await_x(t):
         quad, xs = t // (NX - 1), (x + near_first(t % (NX - 1) + 1) + NX) % NX
@@ -299,14 +288,20 @@
 
     with jax.named_scope("slabs"):
 
-        @pl.loop(0, n_quads - 1)
+        @pl.loop(0, (n_quads - 1) // 2)
         def _(t):
-            add_quad(*await_x(t))
-
-        build(*await_x(n_quads - 1))
-        add_side(1 - c)
+            build(0, *await_x(2 * t))
+            build(1, *await_x(2 * t + 1))
+            add_both(2)
+
+        for t in range((n_quads - 1) // 2 * 2, n_quads - 1):
+            build(0, *await_x(t))
+            add_both(1)
+
+        build(0, *await_x(n_quads - 1))
+        add_side(1, 1 - c)
         swap.start()
-        add_side(c)
+        add_side(1, c)
 
     with jax.named_scope("cores"):
         swap.wait_recv()
@@ -352,14 +347,19 @@
         for f in range(GROUP):
             counts = jnp.where(lane // BINS == f, nbins_ref[z * GROUP + f], counts)
         gain = jnp.where(lane % BINS < counts - 1, gain, 0.0)
+        best = jnp.broadcast_to(jnp.max(gain, axis=1, keepdims=True), (LEAVES, LANES))
         for i in range(NZ):
             gain_s[i] = gain[i * LP : (i + 1) * LP]
+            peak_s[i] = best[i * LP : (i + 1) * LP]
 
     def gain_copy(t):
         other = (z + far_first(t, NZ)) % NZ
         return remote(gain_s.at[other], gain_r.at[z], gain_sem.at[0], gain_sem.at[1], dev(x, y, other, c))
 
-    pair = remote(pair_s, pair_r, pair_sem.at[0], pair_sem.at[1], dev(x, y, z, 1 - c))
+    def peak_copy(t):
+        other = (z + far_first(t, NZ)) % NZ
+        return remote(peak_s.at[other], peak_r.at[z], peak_sem.at[0], peak_sem.at[1], dev(x, y, other, 1 - c))
+
     plane = [(i, j) for i in range(NX) for j in range(NY) if i or j]
     plane.sort(key=lambda step: -min(step[0], NX - step[0]) - min(step[1], NY - step[1]))
     here = x * NY + y
@@ -373,18 +373,16 @@
 
         @pl.loop(0, NZ - 1)
         def _(t):
+            peak_copy(t).start()
             gain_copy(t).start()
 
+        peak_copy(NZ - 1).start()
         gain_r[z] = gain_s[z]
 
         await_bytes(gain_r.at[pl.ds(0, NZ - 1)], gain_sem.at[1])
+        await_bytes(peak_r, peak_sem.at[1])
         best = jnp.max(functools.reduce(jnp.maximum, [gain_r[i] for i in range(NZ)]), axis=1, keepdims=True)
-        pair_s[...] = jnp.broadcast_to(best, (LP, LANES))
-
-    with jax.named_scope("pair"):
-        pair.start()
-        pair.wait_recv()
-        best_s[...] = jnp.maximum(pair_s[...], pair_r[...])
+        best_s[...] = functools.reduce(jnp.maximum, [peak_r[i] for i in range(NZ)] + [best])
 
     with jax.named_scope("plane"):
         for t in range(NX * NY - 1):
@@ -406,7 +404,7 @@
         await_bytes(vals.at[0, pl.ds(0, NY - 1)], send_sem.at[2])
         await_bytes(vals.at[pl.ds(0, NX - 1)], send_sem.at[3])
         swap.wait_send()
-        pair.wait_send()
+        await_bytes(peak_s, peak_sem.at[0])
         await_bytes(gain_s.at[pl.ds(0, NZ - 1)], gain_sem.at[0])
         await_bytes(best_r.at[pl.ds(0, NX * NY - 1)], best_sem.at[0])
 
@@ -422,8 +420,7 @@
     VMEM, DMA = pltpu.VMEM, pltpu.SemaphoreType.DMA
     vmem = pl.BlockSpec(memory_space=pltpu.VMEM)
     hbm = pl.BlockSpec(memory_space=pl.ANY)
-    half = NX * NY // 2
-    bin_block = (GROUP * NX, (NY + 1) * LANES)
+    bin_block = (GROUP * NX, NY * LANES)
     return pl.pallas_call(
         functools.partial(kernel, NX, NY, NZ),
         out_shape=jax.ShapeDtypeStruct((LP, NZ * cols), f32),
@@ -435,24 +432,23 @@
             VMEM((K, classes), bf16),
             VMEM(bins.shape, jnp.int32),
             pltpu.SMEM(nbins.shape, jnp.int32),
-            VMEM((2 * half, LANES), jnp.int32),
+            VMEM((NX * NY, LANES), jnp.int32),
             VMEM((2 * rows, classes), bf16),
             VMEM((NZ, *bin_block), bf16),
-            VMEM((K, 2 * LANES), bf16),
+            VMEM((K, LANES), bf16),
             VMEM((NZ, *bin_block), bf16),
-            VMEM((NZ, K, 2 * LANES), bf16),
+            VMEM((NZ, K, LANES), bf16),
             VMEM((NZ, NY, GROUP * NX, LANES), f32),
-            VMEM((HZ, 2 * half, LANES), f32),
             VMEM((NX, NY, K, span + LANES), bf16),
-            VMEM((tall, QUAD * span), bf16),
-            VMEM((2, cols, QUAD * span), bf16),
+            VMEM((tall, 2 * QUAD * span), bf16),
+            VMEM((2, cols, 2 * QUAD * span), bf16),
             VMEM((2, tall, cols), f32),
             VMEM((tall, cols), f32),
             VMEM((2, cols // LANES, tall, LANES), f32),
             VMEM((NZ, LP, cols), f32),
             VMEM((NZ, LP, cols), f32),
-            VMEM((LP, LANES), f32),
-            VMEM((LP, LANES), f32),
+            VMEM((NZ, LP, LANES), f32),
+            VMEM((NZ, LP, LANES), f32),
             VMEM((LP, LANES), f32),
             VMEM((NX * NY, LP, LANES), f32),
             DMA((6,)),
@@ -477,7 +473,7 @@
         projection.T,
         bins,
         nbins,
-        leaf.reshape(2 * half, LANES),
+        leaf.reshape(NX * NY, LANES),
     )
 
 

time: 51.3 us -> 51.2 us (level)
  no operation moved by 1% of the time
where the time goes in v4:
time: 51.2 us; the launch traced here: 51.1 us
  Pallas kernels  49.7 us (97%)
  local copies, waits for them, and re-layouts  1.32 us (3%)
    pallas_call x1, Pallas kernels, on_device(): pl.pallas_call(functools.partial(kernel, NX, NY, NZ), out_shape=jax.Shape...  49.7 us
    unnamed x1, local copies, waits for them, and re-layouts  1.32 us

profile of v4, /device:TPU:1, one launch (start us, length us, event | category | flops | bytes accessed | tf_op | source)
XLA Modules:
  0.0 51.1 jit_solution(9139814570589536614)
XLA Ops:
  0.0 49.7 %shard_map.64 = f32[2,2048]{1,0:T(2,128)} custom-call(bf16[64,1000]{1,0:T(8,128)(2,1)} %logits_any.1, s32[1,64]{1,0:T(1,128)} %bitcast.5, bf16[16,1000]{1,0:T(8,128)(2,1)} %bitcast.3, s32[32,4096]{1,0:T(8,128)} %bins_any.1, s32[32]{0:T(128)} %nbins_any.1, s32[32,128]{1,0:T(8,128)} %bitcast.4), custom_call_target="tpu_custom_call" | custom-call | flops 4563402752 | bytes 1048576 | tf_op jit(solution)/shard_map/pallas_call | solution.py:424
  49.7 1.3 %copy.8 = f32[2,2048]{1,0:T(2,128)} copy(f32[2,2048]{1,0:T(2,128)} %shard_map.64) | data formatting | bytes 32768

commit v5 on v4

--- a/solution.py
+++ b/solution.py
@@ -11,7 +11,6 @@
 LEAVES = 16
 K = 16
 GROUP = 4
-QUAD = 4
 LANES = 128
 MESH = pl.DeviceIdType.MESH
 NT = (((1,), (1,)), ((), ()))
@@ -54,6 +53,7 @@
     vals,
     weights,
     onehot,
+    steps,
     acc,
     hist_r,
     sums,
@@ -67,7 +67,9 @@
     column_sem,
     send_sem,
     y_sem,
-    x_sem,
+    direct_sem,
+    near_sem,
+    far_sem,
     swap_sem,
     gain_sem,
     peak_sem,
@@ -75,6 +77,8 @@
 ):
     HZ = NZ // 2
     LP = LEAVES // NZ
+    NEAR = NY // 2
+    cols = GROUP * BINS
     rows = labels_ref.shape[1]
     z = lax.axis_index("row")
     feat = lax.axis_index("feat")
@@ -155,6 +159,12 @@
                 [four[:, i * width : (i + 1) * width] for i in range(NX)], axis=0
             ).astype(jnp.bfloat16)
 
+        src = lax.broadcasted_iota(jnp.int32, (cols, cols), 0)
+        dst = lax.broadcasted_iota(jnp.int32, (cols, cols), 1)
+        same = (src // BINS) == (dst // BINS)
+        steps[0] = jnp.where(same & (src <= dst), 1.0, 0.0).astype(jnp.bfloat16)
+        steps[1] = jnp.where(same & (src > dst), 1.0, 0.0).astype(jnp.bfloat16)
+
     with jax.named_scope("barrier"):
         pl.semaphore_wait(barrier, 2 * NZ - 1 + NY - 1 + NX - 1)
 
@@ -208,35 +218,58 @@
         device = dev(x, (y + far_first(t, NY)) % NY, z, c)
         return remote(vals.at[x, y], vals.at[x, y], send_sem.at[2], y_sem.at[y], device)
 
-    def x_copy(t, ys, quad):
+    def x_copy(t, ys, sem):
         device = dev((x + far_first(t, NX)) % NX, y, z, c)
-        return remote(vals.at[x, ys], vals.at[x, ys], send_sem.at[3], x_sem.at[x, quad], device)
-
-    def forward(ys, quad):
-        @pl.loop(0, NX - 1)
-        def _(t):
-            x_copy(t, ys, quad).start()
+        return remote(vals.at[x, ys], vals.at[x, ys], send_sem.at[3], sem.at[x], device)
+
+    def near_y(t):
+        return (y + near_first(t) + NY) % NY
+
+    def near_x(t):
+        return (x + near_first(t) + NX) % NX
+
+    @pl.loop(0, NX - 1)
+    def _(t):
+        x_copy(t, y, direct_sem).start()
 
     @pl.loop(0, NY - 1)
     def _(t):
         y_copy(t).start()
 
-    forward(y, 0)
     acc[...] = jnp.zeros_like(acc)
 
-    def near_y(t):
-        return (y + near_first(t) + NY) % NY
+    @pl.loop(1, NX)
+    def _(i):
+        xs = near_x(i)
+        await_bytes(vals.at[xs, y], direct_sem.at[xs])
+
+        @pl.loop(1, NEAR + 1)
+        def _(t):
+            block = vals.at[xs, y]
+            remote(block, block, send_sem.at[3], near_sem.at[xs], dev(x, near_y(t), z, c)).start()
 
     def await_y(t):
         ys = near_y(t)
         await_bytes(vals.at[x, ys], y_sem.at[ys])
-        forward(ys, t // QUAD)
-
-    pl.loop(1, NY)(await_y)
+        return ys
+
+    @pl.loop(NEAR + 1, NY)
+    def _(i):
+        ys = await_y(i)
+
+        @pl.loop(0, NX - 1)
+        def _(t):
+            x_copy(t, ys, far_sem).start()
+
+    @pl.loop(1, NEAR + 1)
+    def _(i):
+        await_y(i)
 
     with jax.named_scope("zbins"):
         await_bytes(bins_r, column_sem.at[1])
-        for i in range(2 * HZ):
+
+        @pl.loop(0, 2 * HZ)
+        def _(i):
             for j in range(NY):
                 bins_f[i, j] = bins_r[i, :, j * LANES : (j + 1) * LANES].astype(jnp.float32)
 
@@ -244,13 +277,13 @@
     leaf_ids = lax.broadcasted_iota(jnp.int32, (LEAVES, LANES), 0).astype(jnp.float32).astype(jnp.bfloat16)
     one, nil = jnp.bfloat16(1), jnp.bfloat16(0)
 
-    def build(part, xs, quad):
-        for b in range(QUAD):
-            ys = near_y(quad * QUAD + b)
+    def add_blocks(xs, start, count):
+        for b in range(count):
+            ys = near_y(start + b)
             beside = vals[xs, ys, :, HZ * LANES :].astype(jnp.float32)
             for i in range(HZ):
                 src = slice(i * LANES, (i + 1) * LANES)
-                at = ((part * QUAD + b) * HZ + i) * LANES
+                at = (b * HZ + i) * LANES
                 dst = slice(at, at + LANES)
                 hess = jnp.broadcast_to(beside[i : i + 1], (LEAVES, LANES)).astype(jnp.bfloat16)
                 leaf = jnp.broadcast_to(beside[HZ + i : HZ + i + 1], (LEAVES, LANES)).astype(jnp.bfloat16)
@@ -258,70 +291,50 @@
                 for l in range(LEAVES):
                     weights[l * K : (l + 1) * K, dst] = jnp.where(leaf == jnp.bfloat16(l), tile, nil)
                 weights[LEAVES * K :, dst] = jnp.where(leaf == leaf_ids, hess, nil)
-                for side in range(2):
+                for side, core in enumerate((1 - c, c)):
                     for f in range(GROUP):
-                        ids = bins_f[2 * i + side, ys, pl.ds(xs * GROUP + f, 1), :]
+                        ids = bins_f[2 * i + core, ys, pl.ds(xs * GROUP + f, 1), :]
                         ids = jnp.broadcast_to(ids, (BINS, LANES)).astype(jnp.bfloat16)
                         onehot[side, f * BINS : (f + 1) * BINS, dst] = jnp.where(ids == bin_ids, one, nil)
-
-    def add_side(parts, side):
-        depth = slice(0, parts * QUAD * HZ * LANES)
-        acc[side] += lax.dot_general(weights[:, depth], onehot[side, :, depth], NT, preferred_element_type=jnp.float32)
-
-    def add_both(parts):
-        add_side(parts, 0)
-        add_side(parts, 1)
-
-    with jax.named_scope("ownslab"):
-        for quad in range(NY // QUAD):
-            build(quad, x, quad)
-        add_both(NY // QUAD)
-
-    def await_x(t):
-        quad, xs = t // (NX - 1), (x + near_first(t % (NX - 1) + 1) + NX) % NX
-
-        await_bytes(vals.at[xs, pl.ds(0, QUAD)], x_sem.at[xs, quad])
-        return xs, quad
-
-    swap = remote(acc.at[1 - c], hist_r, swap_sem.at[0], swap_sem.at[1], dev(x, y, z, 1 - c))
-    n_quads = (NX - 1) * (NY // QUAD)
+        depth = slice(0, count * HZ * LANES)
+        for side in range(2):
+            acc[side] += lax.dot_general(
+                weights[:, depth], onehot[side, :, depth], NT, preferred_element_type=jnp.float32
+            )
 
     with jax.named_scope("slabs"):
 
-        @pl.loop(0, (n_quads - 1) // 2)
+        @pl.loop(0, NY // NEAR)
         def _(t):
-            build(0, *await_x(2 * t))
-            build(1, *await_x(2 * t + 1))
-            add_both(2)
-
-        for t in range((n_quads - 1) // 2 * 2, n_quads - 1):
-            build(0, *await_x(t))
-            add_both(1)
-
-        build(0, *await_x(n_quads - 1))
-        add_side(1, 1 - c)
-        swap.start()
-        add_side(1, c)
-
+            add_blocks(x, t * NEAR, NEAR)
+
+        @pl.loop(1, NX)
+        def _(i):
+            xs = near_x(i)
+            await_bytes(vals.at[xs, pl.ds(0, NEAR)], near_sem.at[xs])
+            add_blocks(xs, 0, NEAR + 1)
+
+        @pl.loop(1, NX)
+        def _(i):
+            xs = near_x(i)
+            await_bytes(vals.at[xs, pl.ds(0, NY - 1 - NEAR)], far_sem.at[xs])
+            add_blocks(xs, NEAR + 1, NY - 1 - NEAR)
+
+    swap = remote(acc.at[0], hist_r, swap_sem.at[0], swap_sem.at[1], dev(x, y, z, 1 - c))
+    swap.start()
     with jax.named_scope("cores"):
         swap.wait_recv()
 
     with jax.named_scope("gains"):
-        hist = acc[c] + hist_r[...]
-        cols = GROUP * BINS
-        src = lax.broadcasted_iota(jnp.int32, (cols, cols), 0)
-        dst = lax.broadcasted_iota(jnp.int32, (cols, cols), 1)
-        same = (src // BINS) == (dst // BINS)
-        upto = jnp.where(same & (src <= dst), 1.0, 0.0).astype(jnp.bfloat16)
-        past = jnp.where(same & (src > dst), 1.0, 0.0).astype(jnp.bfloat16)
+        hist = acc[1] + hist_r[...]
         left = jnp.zeros_like(hist)
         right = jnp.zeros_like(hist)
         rest = hist
         for _ in range(3):
             piece = rest.astype(jnp.bfloat16)
             rest = rest - piece.astype(jnp.float32)
-            left += jnp.dot(piece, upto, preferred_element_type=jnp.float32)
-            right += jnp.dot(piece, past, preferred_element_type=jnp.float32)
+            left += jnp.dot(piece, steps[0], preferred_element_type=jnp.float32)
+            right += jnp.dot(piece, steps[1], preferred_element_type=jnp.float32)
         for i in range(cols // LANES):
             sums[0, i] = left[:, i * LANES : (i + 1) * LANES]
             sums[1, i] = right[:, i * LANES : (i + 1) * LANES]
@@ -389,13 +402,6 @@
             best_copy(t).start()
         best_r[here] = best_s[...]
 
-        await_bytes(best_r.at[pl.ds(0, NX * NY - 1)], best_sem.at[1])
-        best = functools.reduce(jnp.maximum, [best_r[i] for i in range(NX * NY)])[:, :1]
-        for i in range(NZ):
-            out_ref[:, i * cols : (i + 1) * cols] = gain_r[i] / (best + epsilon)
-
-    with jax.named_scope("sends"):
-
         @pl.loop(0, NZ)
         def _(t):
             column_values(t, "wait")
@@ -406,6 +412,12 @@
         swap.wait_send()
         await_bytes(peak_s, peak_sem.at[0])
         await_bytes(gain_s.at[pl.ds(0, NZ - 1)], gain_sem.at[0])
+
+        await_bytes(best_r.at[pl.ds(0, NX * NY - 1)], best_sem.at[1])
+        best = functools.reduce(jnp.maximum, [best_r[i] for i in range(NX * NY)])[:, :1]
+        for i in range(NZ):
+            out_ref[:, i * cols : (i + 1) * cols] = gain_r[i] / (best + epsilon)
+
         await_bytes(best_r.at[pl.ds(0, NX * NY - 1)], best_sem.at[0])
 
 
@@ -440,8 +452,9 @@
             VMEM((NZ, K, LANES), bf16),
             VMEM((NZ, NY, GROUP * NX, LANES), f32),
             VMEM((NX, NY, K, span + LANES), bf16),
-            VMEM((tall, 2 * QUAD * span), bf16),
-            VMEM((2, cols, 2 * QUAD * span), bf16),
+            VMEM((tall, (NY // 2 + 1) * span), bf16),
+            VMEM((2, cols, (NY // 2 + 1) * span), bf16),
+            VMEM((2, cols, cols), bf16),
             VMEM((2, tall, cols), f32),
             VMEM((tall, cols), f32),
             VMEM((2, cols // LANES, tall, LANES), f32),
@@ -455,7 +468,9 @@
             DMA((2,)),
             DMA((4,)),
             DMA((NY,)),
-            DMA((NX, NY // QUAD)),
+            DMA((NX,)),
+            DMA((NX,)),
+            DMA((NX,)),
             DMA((2,)),
             DMA((2,)),
             DMA((2,)),

time: 51.2 us -> 47.1 us (0.920)
  Pallas kernels: 49.7 us -> 45.6 us
    pallas_call x1, Pallas kernels: 49.7 us -> 45.6 us  [on_device(): pl.pallas_call(functools.partial(kernel, NX, NY, NZ), out_shape=jax.Shape...]
where the time goes in v5:
time: 47.1 us; the launch traced here: 46.9 us
  Pallas kernels  45.6 us (97%)
  local copies, waits for them, and re-layouts  1.32 us (3%)
    pallas_call x1, Pallas kernels, on_device(): pl.pallas_call(functools.partial(kernel, NX, NY, NZ), out_shape=jax.Shape...  45.6 us
    unnamed x1, local copies, waits for them, and re-layouts  1.32 us

profile of v5, /device:TPU:1, one launch (start us, length us, event | category | flops | bytes accessed | tf_op | source)
XLA Modules:
  0.0 46.9 jit_solution(3238701245104035298)
XLA Ops:
  0.0 45.6 %shard_map.64 = f32[2,2048]{1,0:T(2,128)} custom-call(bf16[64,1000]{1,0:T(8,128)(2,1)} %logits_any.1, s32[1,64]{1,0:T(1,128)} %bitcast.5, bf16[16,1000]{1,0:T(8,128)(2,1)} %bitcast.3, s32[32,4096]{1,0:T(8,128)} %bins_any.1, s32[32]{0:T(128)} %nbins_any.1, s32[32,128]{1,0:T(8,128)} %bitcast.4), custom_call_target="tpu_custom_call" | custom-call | flops 4563402752 | bytes 1048576 | tf_op jit(solution)/shard_map/pallas_call | solution.py:436
  45.6 1.3 %copy.8 = f32[2,2048]{1,0:T(2,128)} copy(f32[2,2048]{1,0:T(2,128)} %shard_map.64) | data formatting | bytes 32768

commit v6 on v5

--- a/solution.py
+++ b/solution.py
@@ -277,7 +277,9 @@
     leaf_ids = lax.broadcasted_iota(jnp.int32, (LEAVES, LANES), 0).astype(jnp.float32).astype(jnp.bfloat16)
     one, nil = jnp.bfloat16(1), jnp.bfloat16(0)
 
-    def add_blocks(xs, start, count):
+    swap = remote(acc.at[0], hist_r, swap_sem.at[0], swap_sem.at[1], dev(x, y, z, 1 - c))
+
+    def add_blocks(xs, start, count, last=False):
         for b in range(count):
             ys = near_y(start + b)
             beside = vals[xs, ys, :, HZ * LANES :].astype(jnp.float32)
@@ -298,6 +300,8 @@
                         onehot[side, f * BINS : (f + 1) * BINS, dst] = jnp.where(ids == bin_ids, one, nil)
         depth = slice(0, count * HZ * LANES)
         for side in range(2):
+            if side == 1 and last:
+                swap.start()
             acc[side] += lax.dot_general(
                 weights[:, depth], onehot[side, :, depth], NT, preferred_element_type=jnp.float32
             )
@@ -314,14 +318,14 @@
             await_bytes(vals.at[xs, pl.ds(0, NEAR)], near_sem.at[xs])
             add_blocks(xs, 0, NEAR + 1)
 
-        @pl.loop(1, NX)
-        def _(i):
+        def add_far(i, last=False):
             xs = near_x(i)
             await_bytes(vals.at[xs, pl.ds(0, NY - 1 - NEAR)], far_sem.at[xs])
-            add_blocks(xs, NEAR + 1, NY - 1 - NEAR)
-
-    swap = remote(acc.at[0], hist_r, swap_sem.at[0], swap_sem.at[1], dev(x, y, z, 1 - c))
-    swap.start()
+            add_blocks(xs, NEAR + 1, NY - 1 - NEAR, last)
+
+        pl.loop(1, NX - 1)(add_far)
+        add_far(NX - 1, True)
+
     with jax.named_scope("cores"):
         swap.wait_recv()
 

time: 47.1 us -> 47 us (level)
  no operation moved by 1% of the time
where the time goes in v6:
time: 47 us; the launch traced here: 46.9 us
  Pallas kernels  45.5 us (97%)
  local copies, waits for them, and re-layouts  1.32 us (3%)
    pallas_call x1, Pallas kernels, on_device(): pl.pallas_call(functools.partial(kernel, NX, NY, NZ), out_shape=jax.Shape...  45.5 us
    unnamed x1, local copies, waits for them, and re-layouts  1.32 us

profile of v6, /device:TPU:1, one launch (start us, length us, event | category | flops | bytes accessed | tf_op | source)
XLA Modules:
  0.0 46.9 jit_solution(2025341602154435567)
XLA Ops:
  0.0 45.5 %shard_map.64 = f32[2,2048]{1,0:T(2,128)} custom-call(bf16[64,1000]{1,0:T(8,128)(2,1)} %logits_any.1, s32[1,64]{1,0:T(1,128)} %bitcast.5, bf16[16,1000]{1,0:T(8,128)(2,1)} %bitcast.3, s32[32,4096]{1,0:T(8,128)} %bins_any.1, s32[32]{0:T(128)} %nbins_any.1, s32[32,128]{1,0:T(8,128)} %bitcast.4), custom_call_target="tpu_custom_call" | custom-call | flops 4563402752 | bytes 1048576 | tf_op jit(solution)/shard_map/pallas_call | solution.py:440
  45.5 1.3 %copy.8 = f32[2,2048]{1,0:T(2,128)} copy(f32[2,2048]{1,0:T(2,128)} %shard_map.64) | data formatting | bytes 32768
